TPU v7x, 1024 devices: a whole 8x8x8 slice. The times are simulated.
1024 devices in a mesh: blk: 16 (over z, x_lo), group: 64 (over y, x_hi, core).
Axes of the slice: x: 8 (x_hi: 4, x_lo: 2; x = x_hi * 2 + x_lo), y: 8, z: 8, core: 2. Of those that a mesh axis runs over, the one named last changes fastest.
Arguments:
- tokens: bfloat16 [49152, 6, 1152], P(('blk', 'group')), may hold values from -24 to 24
- lengths: int32 [49152], P(('blk', 'group')), may hold values from 1 to 6
- caption_ids: int32 [49152], P(('blk', 'group')), may hold values from 0 to 1023
- destination: int32 [49152], P(('blk', 'group')), may hold values from 0 to 63, as said below
- slot: int32 [49152], P(('blk', 'group')), may hold values from 0 to 1
- images: bfloat16 [131072, 1152], P(('blk', 'group')), may hold values from -24 to 24
- image_ids: int32 [131072], P(('blk', 'group')), may hold values from 0 to 1023
- head_weight: bfloat16 [1152, 1152], replicated, may hold values from -1 to 2
- logit_scale: float32 [1], replicated, may hold values from 4 to 12
- logit_bias: float32 [1], replicated, may hold values from -3 to -1
Outputs:
- image_grad: float32 [131072, 1152], P(('blk', 'group'))
- text_grad: float32 [131072, 1152], P(('blk', 'group'))
- row_loss: float32 [131072], P(('blk', 'group'))
Inputs may be any that keep to these rules, and one draw needn't show every extreme that they name: On one device no two captions share a destination and a slot.
All inputs are finite; a program needn't handle non-finite values.
Results may differ from a plain program's by a relative error of at most 0.0044.
Values may be sent and summed in bfloat16 or wider, within the bound.
A program may use at most 64 MiB of HBM per device.

v0:
```python
import jax
import jax.numpy as jnp
from jax import lax
from jax.sharding import PartitionSpec as P

D = 1152
TXT_DEV = 128


NORM_EPS = 1e-06


def from_behind(array, axis, by):
    peers = lax.axis_size(axis)
    return lax.ppermute(array, axis, [(i, (i + by) % peers) for i in range(peers)])


def pool_rows(token_block, counts):
    live = (jnp.arange(token_block.shape[1], dtype=jnp.int32)[None, :] < counts[:, None]).astype(
        jnp.bfloat16
    )
    summed = jnp.einsum("nl,nld->nd", live, token_block, preferred_element_type=jnp.float32)
    return summed / jnp.maximum(counts, 1).astype(jnp.float32)[:, None]


def pair_weights(image_b, image_ids, block, block_ids, scale_value, bias_value):
    products = lax.dot_general(
        image_b, block, (((1,), (1,)), ((), ())), preferred_element_type=jnp.float32
    )
    logits = scale_value * products + bias_value
    signs = jnp.where(image_ids[:, None] == block_ids[None, :], 1.0, -1.0).astype(jnp.float32)
    live = (block_ids >= 0).astype(jnp.float32)[None, :]
    flipped = -signs * logits
    weights = (live * -signs * jax.nn.sigmoid(flipped) * scale_value).astype(jnp.bfloat16)
    return (weights, live, flipped)


def pair_terms(image_b, image_ids, block, block_ids, scale_value, bias_value):
    weights, live, flipped = pair_weights(
        image_b, image_ids, block, block_ids, scale_value, bias_value
    )
    loss_part = jnp.sum(live * jax.nn.softplus(flipped), axis=1)
    return (weights, loss_part)


def text_terms(weights, image_block):
    return lax.dot_general(
        weights, image_block, (((0,), (0,)), ((), ())), preferred_element_type=jnp.float32
    )


def per_device(
    tokens,
    lengths,
    caption_ids,
    destination,
    slot,
    images,
    image_ids,
    head_weight,
    logit_scale,
    logit_bias,
):
    groups = lax.axis_size("group")
    loop_size = lax.axis_size("blk")
    reach_steps = min(4, (loop_size - 1) // 2)
    text_slots = TXT_DEV
    per_source = text_slots // groups
    position = destination * per_source + slot
    send_ids = jnp.full((text_slots,), -1, jnp.int32).at[position].set(caption_ids)
    pooled_here = pool_rows(tokens, lengths).astype(jnp.bfloat16)
    send_pooled = jnp.zeros((text_slots, D), jnp.bfloat16).at[position].set(pooled_here)
    pooled_b, got_ids = (
        lax.all_to_all(send_pooled, "group", split_axis=0, concat_axis=0, tiled=True),
        lax.all_to_all(send_ids, "group", split_axis=0, concat_axis=0, tiled=True),
    )
    raw = jnp.dot(pooled_b, head_weight, preferred_element_type=jnp.float32)
    text_factor = lax.rsqrt(jnp.sum(raw * raw, axis=-1, keepdims=True) + NORM_EPS)
    text_norm = raw * text_factor
    text_b = text_norm.astype(jnp.bfloat16)
    image_f = images.astype(jnp.float32)
    image_factor = lax.rsqrt(jnp.sum(image_f * image_f, axis=-1, keepdims=True) + NORM_EPS)
    image_norm = image_f * image_factor
    image_b = image_norm.astype(jnp.bfloat16)
    scale_value = logit_scale[0]
    bias_value = logit_bias[0]
    weights, loss_rows = pair_terms(image_b, image_ids, text_b, got_ids, scale_value, bias_value)
    image_sum = jnp.dot(weights, text_b, preferred_element_type=jnp.float32)
    text_sum = text_terms(weights, image_b)
    ahead_block, ahead_ids = (text_b, got_ids)
    behind_block, behind_ids = (text_b, got_ids)
    for distance in range(1, reach_steps + 1):
        ahead_block, ahead_ids = from_behind((ahead_block, ahead_ids), "blk", 1)
        weights, loss_part = pair_terms(
            image_b, image_ids, ahead_block, ahead_ids, scale_value, bias_value
        )
        loss_rows = loss_rows + loss_part
        image_sum = image_sum + jnp.dot(weights, ahead_block, preferred_element_type=jnp.float32)
        text_part = text_terms(weights, image_b)
        text_sum = text_sum + from_behind(text_part, "blk", -distance)
        behind_block, behind_ids = from_behind((behind_block, behind_ids), "blk", -1)
        weights, loss_part = pair_terms(
            image_b, image_ids, behind_block, behind_ids, scale_value, bias_value
        )
        loss_rows = loss_rows + loss_part
        image_sum = image_sum + jnp.dot(weights, behind_block, preferred_element_type=jnp.float32)
        text_part = text_terms(weights, image_b)
        text_sum = text_sum + from_behind(text_part, "blk", distance)
    image_grad = image_factor * (
        image_sum - image_norm * jnp.sum(image_norm * image_sum, axis=-1, keepdims=True)
    )
    text_raw_grad = text_factor * (
        text_sum - text_norm * jnp.sum(text_norm * text_sum, axis=-1, keepdims=True)
    )
    text_grad = lax.dot_general(
        text_raw_grad.astype(jnp.bfloat16),
        head_weight,
        (((1,), (1,)), ((), ())),
        preferred_element_type=jnp.float32,
    )
    return (image_grad, text_grad, loss_rows)


def solution(mesh):
    return jax.shard_map(
        per_device,
        mesh=mesh,
        in_specs=(
            P(("blk", "group"), None, None),
            P(("blk", "group")),
            P(("blk", "group")),
            P(("blk", "group")),
            P(("blk", "group")),
            P(("blk", "group"), None),
            P(("blk", "group")),
            P(),
            P(),
            P(),
        ),
        out_specs=(P(("blk", "group"), None), P(("blk", "group"), None), P(("blk", "group"))),
        check_vma=False,
    )
```

profile of v0, /device:TPU:6, one launch (start us, length us, event | category | flops | bytes accessed | tf_op | source)
XLA Modules:
  0.0 235.3 jit_solution(9456798953629975607)
XLA Ops:
  3.1 12.6 %all-to-all-start = ((s32[64,2,1]{1,2,0:T(1,128)}), s32[64,2,1]{1,2,0:T(1,128)S(1)}, u32[]{:S(2)}, u32[]{:S(2)}) async-start(s32[64,2,1]{1,2,0:T(1,128)} %bitcast), calls=%async_computation | async-start | bytes 65536 | tf_op jit(solution)/shard_map/all_to_all | solution.py:75
  22.2 3.6 %all-to-all-done = s32[64,2,1]{1,2,0:T(1,128)S(1)} async-done(((s32[64,2,1]{1,2,0:T(1,128)}), s32[64,2,1]{1,2,0:T(1,128)S(1)}, u32[]{:S(2)}, u32[]{:S(2)}) %all-to-all-start) | async-done | bytes 544 | tf_op jit(solution)/shard_map/all_to_all | solution.py:75
  25.8 9.1 %all-to-all-start.1 = ((bf16[64,2,1152]{2,1,0:T(2,128)(2,1)}), bf16[64,2,1152]{2,1,0:T(2,128)(2,1)S(1)}, u32[]{:S(2)}, u32[]{:S(2)}) async-start(bf16[64,2,1152]{2,1,0:T(2,128)(2,1)} %all_to_all.19), calls=%async_computation.1 | async-start | bytes 589824 | tf_op jit(solution)/shard_map/all_to_all | solution.py:74
  36.3 7.1 %collective-permute-start.2 = (s32[128]{0:T(128)S(1)}, s32[128]{0:T(128)S(1)}, u32[]{:S(2)}, u32[]{:S(2)}) collective-permute-start(s32[128]{0:T(128)S(1)} %all_to_all.18), channel_id=1, source_target_pairs={{0,960},{64,0},{128,64},{192,128},{256,192},{320,256},{384,320},{4... | collective-permute-start | bytes 1544 | tf_op jit(solution)/shard_map/ppermute | solution.py:15
  46.5 13.6 %collective-permute-start.6 = (s32[128]{0:T(128)S(1)}, s32[128]{0:T(128)S(1)}, u32[]{:S(2)}, u32[]{:S(2)}) collective-permute-start(s32[128]{0:T(128)S(1)} %collective-permute-done.2), channel_id=1, source_target_pairs={{0,960},{64,0},{128,64},{192,128},{256,192},{320,256},{384,320},{4... | collective-permute-start | bytes 1544 | tf_op jit(solution)/shard_map/ppermute | solution.py:15
  63.2 6.0 %collective-permute-start.10 = (s32[128]{0:T(128)S(1)}, s32[128]{0:T(128)S(1)}, u32[]{:S(2)}, u32[]{:S(2)}) collective-permute-start(s32[128]{0:T(128)S(1)} %collective-permute-done.6), channel_id=1, source_target_pairs={{0,960},{64,0},{128,64},{192,128},{256,192},{320,256},{384,320},{4... | collective-permute-start | bytes 1544 | tf_op jit(solution)/shard_map/ppermute | solution.py:15
  72.3 6.0 %collective-permute-start.14 = (s32[128]{0:T(128)S(1)}, s32[128]{0:T(128)S(1)}, u32[]{:S(2)}, u32[]{:S(2)}) collective-permute-start(s32[128]{0:T(128)S(1)} %collective-permute-done.10), channel_id=1, source_target_pairs={{0,960},{64,0},{128,64},{192,128},{256,192},{320,256},{384,320},{4... | collective-permute-start | bytes 1544 | tf_op jit(solution)/shard_map/ppermute | solution.py:15
  81.3 5.1 %collective-permute-done.12 = s32[128]{0:T(128)S(1)} collective-permute-done((s32[128]{0:T(128)S(1)}, s32[128]{0:T(128)S(1)}, u32[]{:S(2)}, u32[]{:S(2)}) %collective-permute-start.12) | collective-permute-done | bytes 544 | tf_op jit(solution)/shard_map/ppermute | solution.py:15
  87.9 6.0 %collective-permute-start.3 = (bf16[128,1152]{1,0:T(8,128)(2,1)S(1)}, bf16[128,1152]{1,0:T(8,128)(2,1)S(1)}, u32[]{:S(2)}, u32[]{:S(2)}) collective-permute-start(bf16[128,1152]{1,0:T(8,128)(2,1)S(1)} %multiply_convert_fusion.1), channel_id=1, source_target_pairs={{0,960},{64,0},{128,64},{192,128},{256,192},{320,256},{384,320},{4... | collective-permute-start | bytes 884744 | tf_op jit(solution)/shard_map/ppermute | solution.py:15
  96.7 8.0 %collective-permute-done.1 = bf16[128,1152]{1,0:T(8,128)(2,1)S(1)} collective-permute-done((bf16[128,1152]{1,0:T(8,128)(2,1)S(1)}, bf16[128,1152]{1,0:T(8,128)(2,1)S(1)}, u32[]{:S(2)}, u32[]{:S(2)}) %collective-permute-start.1) | collective-permute-done | bytes 294944 | tf_op jit(solution)/shard_map/ppermute | solution.py:15
  105.4 2.0 collective-permute-start.16
  108.1 4.8 %collective-permute-start.17 = (f32[128,1152]{1,0:T(8,128)S(1)}, f32[128,1152]{1,0:T(8,128)S(1)}, u32[]{:S(2)}, u32[]{:S(2)}) collective-permute-start(f32[128,1152]{1,0:T(8,128)S(1)} %fusion.69), channel_id=1, source_target_pairs={{0,64},{64,128},{128,192},{192,256},{256,320},{320,384},{384,448},... | collective-permute-start | bytes 1769480 | tf_op jit(solution)/shard_map/ppermute | solution.py:15
  114.9 4.8 %collective-permute-start.5 = (bf16[128,1152]{1,0:T(8,128)(2,1)S(1)}, bf16[128,1152]{1,0:T(8,128)(2,1)S(1)}, u32[]{:S(2)}, u32[]{:S(2)}) collective-permute-start(bf16[128,1152]{1,0:T(8,128)(2,1)S(1)} %collective-permute-done.1), channel_id=1, source_target_pairs={{0,64},{64,128},{128,192},{192,256},{256,320},{320,384},{384,448},... | collective-permute-start | bytes 884744 | tf_op jit(solution)/shard_map/ppermute | solution.py:15
  120.4 21.5 %collective-permute-done.7 = bf16[128,1152]{1,0:T(8,128)(2,1)S(1)} collective-permute-done((bf16[128,1152]{1,0:T(8,128)(2,1)S(1)}, bf16[128,1152]{1,0:T(8,128)(2,1)S(1)}, u32[]{:S(2)}, u32[]{:S(2)}) %collective-permute-start.7) | collective-permute-done | bytes 294944 | tf_op jit(solution)/shard_map/ppermute | solution.py:15
  142.7 2.0 collective-permute-start.19
  144.7 4.4 %collective-permute-start.11 = (bf16[128,1152]{1,0:T(8,128)(2,1)S(1)}, bf16[128,1152]{1,0:T(8,128)(2,1)S(1)}, u32[]{:S(2)}, u32[]{:S(2)}) collective-permute-start(bf16[128,1152]{1,0:T(8,128)(2,1)S(1)} %collective-permute-done.7), channel_id=1, source_target_pairs={{0,960},{64,0},{128,64},{192,128},{256,192},{320,256},{384,320},{4... | collective-permute-start | bytes 884744 | tf_op jit(solution)/shard_map/ppermute | solution.py:15
  149.1 2.4 collective-permute-start.9
  154.7 6.6 %collective-permute-start.18 = (f32[128,1152]{1,0:T(8,128)S(1)}, f32[128,1152]{1,0:T(8,128)S(1)}, u32[]{:S(2)}, u32[]{:S(2)}) collective-permute-start(f32[128,1152]{1,0:T(8,128)S(1)} %fusion.70), channel_id=1, source_target_pairs={{0,896},{64,960},{128,0},{192,64},{256,128},{320,192},{384,256},{4... | collective-permute-start | bytes 1769480 | tf_op jit(solution)/shard_map/ppermute | solution.py:15
  166.3 5.7 %collective-permute-done.15 = bf16[128,1152]{1,0:T(8,128)(2,1)S(1)} collective-permute-done((bf16[128,1152]{1,0:T(8,128)(2,1)S(1)}, bf16[128,1152]{1,0:T(8,128)(2,1)S(1)}, u32[]{:S(2)}, u32[]{:S(2)}) %collective-permute-start.15) | collective-permute-done | bytes 294944 | tf_op jit(solution)/shard_map/ppermute | solution.py:15
  175.1 8.9 %collective-permute-done.13 = bf16[128,1152]{1,0:T(8,128)(2,1)S(1)} collective-permute-done((bf16[128,1152]{1,0:T(8,128)(2,1)S(1)}, bf16[128,1152]{1,0:T(8,128)(2,1)S(1)}, u32[]{:S(2)}, u32[]{:S(2)}) %collective-permute-start.13) | collective-permute-done | bytes 294944 | tf_op jit(solution)/shard_map/ppermute | solution.py:15
  183.9 9.3 %collective-permute-start.21 = (f32[128,1152]{1,0:T(8,128)S(1)}, f32[128,1152]{1,0:T(8,128)S(1)}, u32[]{:S(2)}, u32[]{:S(2)}) collective-permute-start(f32[128,1152]{1,0:T(8,128)S(1)} %fusion.74), channel_id=1, source_target_pairs={{0,192},{64,256},{128,320},{192,384},{256,448},{320,512},{384,576}... | collective-permute-start | bytes 1769480 | tf_op jit(solution)/shard_map/ppermute | solution.py:15
  196.3 8.1 %collective-permute-start.22 = (f32[128,1152]{1,0:T(8,128)S(1)}, f32[128,1152]{1,0:T(8,128)S(1)}, u32[]{:S(2)}, u32[]{:S(2)}) collective-permute-start(f32[128,1152]{1,0:T(8,128)S(1)} %fusion.76), channel_id=1, source_target_pairs={{0,768},{64,832},{128,896},{192,960},{256,0},{320,64},{384,128},{4... | collective-permute-start | bytes 1769480 | tf_op jit(solution)/shard_map/ppermute | solution.py:15
  207.9 6.6 %collective-permute-done.20 = f32[128,1152]{1,0:T(8,128)S(1)} collective-permute-done((f32[128,1152]{1,0:T(8,128)S(1)}, f32[128,1152]{1,0:T(8,128)S(1)}, u32[]{:S(2)}, u32[]{:S(2)}) %collective-permute-start.20) | collective-permute-done | bytes 589856 | tf_op jit(solution)/shard_map/ppermute | solution.py:15
  214.5 18.4 %collective-permute-done.22 = f32[128,1152]{1,0:T(8,128)S(1)} collective-permute-done((f32[128,1152]{1,0:T(8,128)S(1)}, f32[128,1152]{1,0:T(8,128)S(1)}, u32[]{:S(2)}, u32[]{:S(2)}) %collective-permute-start.22) | collective-permute-done | bytes 589856 | tf_op jit(solution)/shard_map/ppermute | solution.py:15
  (135 shorter events, 49.9 us)
Async XLA Ops:
  3.1 22.7 %all-to-all-start = ((s32[64,2,1]{1,2,0:T(1,128)}), s32[64,2,1]{1,2,0:T(1,128)S(1)}, u32[]{:S(2)}, u32[]{:S(2)}) async-start(s32[64,2,1]{1,2,0:T(1,128)} %bitcast), calls=%async_computation | async-start | bytes 65536 | tf_op jit(solution)/shard_map/all_to_all | solution.py:75
  25.8 61.1 %all-to-all-start.1 = ((bf16[64,2,1152]{2,1,0:T(2,128)(2,1)}), bf16[64,2,1152]{2,1,0:T(2,128)(2,1)S(1)}, u32[]{:S(2)}, u32[]{:S(2)}) async-start(bf16[64,2,1152]{2,1,0:T(2,128)(2,1)} %all_to_all.19), calls=%async_computation.1 | async-start | bytes 589824 | tf_op jit(solution)/shard_map/all_to_all | solution.py:74
  36.3 9.6 %collective-permute-start.2 = (s32[128]{0:T(128)S(1)}, s32[128]{0:T(128)S(1)}, u32[]{:S(2)}, u32[]{:S(2)}) collective-permute-start(s32[128]{0:T(128)S(1)} %all_to_all.18), channel_id=1, source_target_pairs={{0,960},{64,0},{128,64},{192,128},{256,192},{320,256},{384,320},{4... | collective-permute-start | bytes 1544 | tf_op jit(solution)/shard_map/ppermute | solution.py:15
  44.0 16.1 %collective-permute-start = (s32[128]{0:T(128)S(1)}, s32[128]{0:T(128)S(1)}, u32[]{:S(2)}, u32[]{:S(2)}) collective-permute-start(s32[128]{0:T(128)S(1)} %all_to_all.18), channel_id=1, source_target_pairs={{0,64},{64,128},{128,192},{192,256},{256,320},{320,384},{384,448},... | collective-permute-start | bytes 1544 | tf_op jit(solution)/shard_map/ppermute | solution.py:15
  46.5 16.1 %collective-permute-start.6 = (s32[128]{0:T(128)S(1)}, s32[128]{0:T(128)S(1)}, u32[]{:S(2)}, u32[]{:S(2)}) collective-permute-start(s32[128]{0:T(128)S(1)} %collective-permute-done.2), channel_id=1, source_target_pairs={{0,960},{64,0},{128,64},{192,128},{256,192},{320,256},{384,320},{4... | collective-permute-start | bytes 1544 | tf_op jit(solution)/shard_map/ppermute | solution.py:15
  60.7 8.6 %collective-permute-start.4 = (s32[128]{0:T(128)S(1)}, s32[128]{0:T(128)S(1)}, u32[]{:S(2)}, u32[]{:S(2)}) collective-permute-start(s32[128]{0:T(128)S(1)} %collective-permute-done), channel_id=1, source_target_pairs={{0,64},{64,128},{128,192},{192,256},{256,320},{320,384},{384,448},... | collective-permute-start | bytes 1544 | tf_op jit(solution)/shard_map/ppermute | solution.py:15
  63.2 8.5 %collective-permute-start.10 = (s32[128]{0:T(128)S(1)}, s32[128]{0:T(128)S(1)}, u32[]{:S(2)}, u32[]{:S(2)}) collective-permute-start(s32[128]{0:T(128)S(1)} %collective-permute-done.6), channel_id=1, source_target_pairs={{0,960},{64,0},{128,64},{192,128},{256,192},{320,256},{384,320},{4... | collective-permute-start | bytes 1544 | tf_op jit(solution)/shard_map/ppermute | solution.py:15
  69.8 8.6 %collective-permute-start.8 = (s32[128]{0:T(128)S(1)}, s32[128]{0:T(128)S(1)}, u32[]{:S(2)}, u32[]{:S(2)}) collective-permute-start(s32[128]{0:T(128)S(1)} %collective-permute-done.4), channel_id=1, source_target_pairs={{0,64},{64,128},{128,192},{192,256},{256,320},{320,384},{384,448},... | collective-permute-start | bytes 1544 | tf_op jit(solution)/shard_map/ppermute | solution.py:15
  87.9 19.5 %collective-permute-start.3 = (bf16[128,1152]{1,0:T(8,128)(2,1)S(1)}, bf16[128,1152]{1,0:T(8,128)(2,1)S(1)}, u32[]{:S(2)}, u32[]{:S(2)}) collective-permute-start(bf16[128,1152]{1,0:T(8,128)(2,1)S(1)} %multiply_convert_fusion.1), channel_id=1, source_target_pairs={{0,960},{64,0},{128,64},{192,128},{256,192},{320,256},{384,320},{4... | collective-permute-start | bytes 884744 | tf_op jit(solution)/shard_map/ppermute | solution.py:15
  94.0 10.7 %collective-permute-start.1 = (bf16[128,1152]{1,0:T(8,128)(2,1)S(1)}, bf16[128,1152]{1,0:T(8,128)(2,1)S(1)}, u32[]{:S(2)}, u32[]{:S(2)}) collective-permute-start(bf16[128,1152]{1,0:T(8,128)(2,1)S(1)} %multiply_convert_fusion.1), channel_id=1, source_target_pairs={{0,64},{64,128},{128,192},{192,256},{256,320},{320,384},{384,448},... | collective-permute-start | bytes 884744 | tf_op jit(solution)/shard_map/ppermute | solution.py:15
  105.4 89.0 %collective-permute-start.16 = (f32[128,1152]{1,0:T(8,128)S(1)}, f32[128,1152]{1,0:T(8,128)S(1)}, u32[]{:S(2)}, u32[]{:S(2)}) collective-permute-start(f32[128,1152]{1,0:T(8,128)S(1)} %fusion.68), channel_id=1, source_target_pairs={{0,960},{64,0},{128,64},{192,128},{256,192},{320,256},{384,320},{4... | collective-permute-start | bytes 1769480 | tf_op jit(solution)/shard_map/ppermute | solution.py:15
  108.1 88.2 %collective-permute-start.17 = (f32[128,1152]{1,0:T(8,128)S(1)}, f32[128,1152]{1,0:T(8,128)S(1)}, u32[]{:S(2)}, u32[]{:S(2)}) collective-permute-start(f32[128,1152]{1,0:T(8,128)S(1)} %fusion.69), channel_id=1, source_target_pairs={{0,64},{64,128},{128,192},{192,256},{256,320},{320,384},{384,448},... | collective-permute-start | bytes 1769480 | tf_op jit(solution)/shard_map/ppermute | solution.py:15
  112.9 29.0 %collective-permute-start.7 = (bf16[128,1152]{1,0:T(8,128)(2,1)S(1)}, bf16[128,1152]{1,0:T(8,128)(2,1)S(1)}, u32[]{:S(2)}, u32[]{:S(2)}) collective-permute-start(bf16[128,1152]{1,0:T(8,128)(2,1)S(1)} %collective-permute-done.3), channel_id=1, source_target_pairs={{0,960},{64,0},{128,64},{192,128},{256,192},{320,256},{384,320},{4... | collective-permute-start | bytes 884744 | tf_op jit(solution)/shard_map/ppermute | solution.py:15
  114.9 34.2 %collective-permute-start.5 = (bf16[128,1152]{1,0:T(8,128)(2,1)S(1)}, bf16[128,1152]{1,0:T(8,128)(2,1)S(1)}, u32[]{:S(2)}, u32[]{:S(2)}) collective-permute-start(bf16[128,1152]{1,0:T(8,128)(2,1)S(1)} %collective-permute-done.1), channel_id=1, source_target_pairs={{0,64},{64,128},{128,192},{192,256},{256,320},{320,384},{384,448},... | collective-permute-start | bytes 884744 | tf_op jit(solution)/shard_map/ppermute | solution.py:15
  142.7 61.8 %collective-permute-start.19 = (f32[128,1152]{1,0:T(8,128)S(1)}, f32[128,1152]{1,0:T(8,128)S(1)}, u32[]{:S(2)}, u32[]{:S(2)}) collective-permute-start(f32[128,1152]{1,0:T(8,128)S(1)} %fusion.71), channel_id=1, source_target_pairs={{0,128},{64,192},{128,256},{192,320},{256,384},{320,448},{384,512}... | collective-permute-start | bytes 1769480 | tf_op jit(solution)/shard_map/ppermute | solution.py:15
  144.7 10.0 %collective-permute-start.11 = (bf16[128,1152]{1,0:T(8,128)(2,1)S(1)}, bf16[128,1152]{1,0:T(8,128)(2,1)S(1)}, u32[]{:S(2)}, u32[]{:S(2)}) collective-permute-start(bf16[128,1152]{1,0:T(8,128)(2,1)S(1)} %collective-permute-done.7), channel_id=1, source_target_pairs={{0,960},{64,0},{128,64},{192,128},{256,192},{320,256},{384,320},{4... | collective-permute-start | bytes 884744 | tf_op jit(solution)/shard_map/ppermute | solution.py:15
  149.1 13.1 %collective-permute-start.9 = (bf16[128,1152]{1,0:T(8,128)(2,1)S(1)}, bf16[128,1152]{1,0:T(8,128)(2,1)S(1)}, u32[]{:S(2)}, u32[]{:S(2)}) collective-permute-start(bf16[128,1152]{1,0:T(8,128)(2,1)S(1)} %collective-permute-done.5), channel_id=1, source_target_pairs={{0,64},{64,128},{128,192},{192,256},{256,320},{320,384},{384,448},... | collective-permute-start | bytes 884744 | tf_op jit(solution)/shard_map/ppermute | solution.py:15
  154.7 53.3 %collective-permute-start.18 = (f32[128,1152]{1,0:T(8,128)S(1)}, f32[128,1152]{1,0:T(8,128)S(1)}, u32[]{:S(2)}, u32[]{:S(2)}) collective-permute-start(f32[128,1152]{1,0:T(8,128)S(1)} %fusion.70), channel_id=1, source_target_pairs={{0,896},{64,960},{128,0},{192,64},{256,128},{320,192},{384,256},{4... | collective-permute-start | bytes 1769480 | tf_op jit(solution)/shard_map/ppermute | solution.py:15
  162.2 9.8 %collective-permute-start.15 = (bf16[128,1152]{1,0:T(8,128)(2,1)S(1)}, bf16[128,1152]{1,0:T(8,128)(2,1)S(1)}, u32[]{:S(2)}, u32[]{:S(2)}) collective-permute-start(bf16[128,1152]{1,0:T(8,128)(2,1)S(1)} %collective-permute-done.11), channel_id=1, source_target_pairs={{0,960},{64,0},{128,64},{192,128},{256,192},{320,256},{384,320},{4... | collective-permute-start | bytes 884744 | tf_op jit(solution)/shard_map/ppermute | solution.py:15
  172.1 11.8 %collective-permute-start.13 = (bf16[128,1152]{1,0:T(8,128)(2,1)S(1)}, bf16[128,1152]{1,0:T(8,128)(2,1)S(1)}, u32[]{:S(2)}, u32[]{:S(2)}) collective-permute-start(bf16[128,1152]{1,0:T(8,128)(2,1)S(1)} %collective-permute-done.9), channel_id=1, source_target_pairs={{0,64},{64,128},{128,192},{192,256},{256,320},{320,384},{384,448},... | collective-permute-start | bytes 884744 | tf_op jit(solution)/shard_map/ppermute | solution.py:15
  183.9 24.0 %collective-permute-start.21 = (f32[128,1152]{1,0:T(8,128)S(1)}, f32[128,1152]{1,0:T(8,128)S(1)}, u32[]{:S(2)}, u32[]{:S(2)}) collective-permute-start(f32[128,1152]{1,0:T(8,128)S(1)} %fusion.74), channel_id=1, source_target_pairs={{0,192},{64,256},{128,320},{192,384},{256,448},{320,512},{384,576}... | collective-permute-start | bytes 1769480 | tf_op jit(solution)/shard_map/ppermute | solution.py:15
  194.4 20.2 %collective-permute-start.20 = (f32[128,1152]{1,0:T(8,128)S(1)}, f32[128,1152]{1,0:T(8,128)S(1)}, u32[]{:S(2)}, u32[]{:S(2)}) collective-permute-start(f32[128,1152]{1,0:T(8,128)S(1)} %fusion.73), channel_id=1, source_target_pairs={{0,832},{64,896},{128,960},{192,0},{256,64},{320,128},{384,192},{4... | collective-permute-start | bytes 1769480 | tf_op jit(solution)/shard_map/ppermute | solution.py:15
  196.3 36.6 %collective-permute-start.22 = (f32[128,1152]{1,0:T(8,128)S(1)}, f32[128,1152]{1,0:T(8,128)S(1)}, u32[]{:S(2)}, u32[]{:S(2)}) collective-permute-start(f32[128,1152]{1,0:T(8,128)S(1)} %fusion.76), channel_id=1, source_target_pairs={{0,768},{64,832},{128,896},{192,960},{256,0},{320,64},{384,128},{4... | collective-permute-start | bytes 1769480 | tf_op jit(solution)/shard_map/ppermute | solution.py:15
  204.5 28.5 %collective-permute-start.23 = (f32[128,1152]{1,0:T(8,128)S(1)}, f32[128,1152]{1,0:T(8,128)S(1)}, u32[]{:S(2)}, u32[]{:S(2)}) collective-permute-start(f32[128,1152]{1,0:T(8,128)S(1)} %fusion.77), channel_id=1, source_target_pairs={{0,256},{64,320},{128,384},{192,448},{256,512},{320,576},{384,640}... | collective-permute-start | bytes 1769480 | tf_op jit(solution)/shard_map/ppermute | solution.py:15
  (28 other events, 664.0 us)
where the time goes:
time: 236 us; the launch traced here: 235 us
  starting transfers between devices  124 us (53%)
  waiting for transfers between devices  80.5 us (34%)
  matrix products  13.7 us (6%)
  other arithmetic  11 us (5%)
  local copies, waits for them, and re-layouts  3.32 us (1%)
  between operations  2.8 us (1%)
    ppermute x24, starting transfers between devices, from_behind(): lax.ppermute(array, axis, [(i, (i + by) % peers) for i in range(peers)])  102 us
    ppermute x24, waiting for transfers between devices, from_behind(): lax.ppermute(array, axis, [(i, (i + by) % peers) for i in range(peers)])  76.9 us
    all_to_all x1, starting transfers between devices, per_device(): lax.all_to_all(send_ids, 'group', split_axis=0, concat_axis=0, tiled=True)  12.6 us
    all_to_all x1, starting transfers between devices, per_device(): lax.all_to_all(send_pooled, 'group', split_axis=0, concat_axis=0, tiled=T...  9.09 us
    convert_element_type x9, other arithmetic, pair_weights(): live = (block_ids >= 0).astype(jnp.float32)[None, :]  4.93 us
  transfers between devices with their start and end apart: 26, of which 10 were waited for; matrix products, arithmetic and copies ran while one was open for 9% of the time, Pallas kernels for 0%

commit v1 on v0

v1 whole, which is shorter than its diff:
```python
import jax
import jax.numpy as jnp
from jax import lax
from jax.experimental import pallas as pl
from jax.experimental.pallas import tpu as pltpu
from jax.sharding import PartitionSpec as P

D = 1152
ROWS = 128
CAPS_HERE = 48
TOKENS = 6
NORM_EPS = 1e-06
HALF = 640
FAN = 8
PIECES = 2
PIECE = ROWS // PIECES
MESH = pl.DeviceIdType.MESH
BF16 = jnp.bfloat16
F32 = jnp.float32


def iota(shape, dim):
    return lax.broadcasted_iota(jnp.int32, shape, dim)


def dot(a, b):
    return lax.dot_general(a, b, (((1,), (0,)), ((), ())), preferred_element_type=F32)


def dot_t(a, b):
    return lax.dot_general(a, b, (((1,), (1,)), ((), ())), preferred_element_type=F32)


def swap_pairs(r):
    return ((r >> 1) & 7) * 16 + (r >> 4) * 2 + (r & 1)


def kernel(
    tokens_hbm,
    lengths_hbm,
    caption_ids_hbm,
    destination_hbm,
    slot_hbm,
    images_hbm,
    image_ids_hbm,
    head_hbm,
    scale_ref,
    bias_ref,
    image_grad_hbm,
    text_grad_hbm,
    loss_hbm,
    tokens,
    meta,
    images,
    image_ids_in,
    head,
    out_image,
    out_text,
    out_loss,
    im_buf,
    im_ids,
    im_peer,
    im_peer_ids,
    tx_buf,
    tx_ids,
    tx_peer,
    tx_peer_ids,
    send_a1,
    recv_a1,
    send_a2,
    recv_a2,
    send_b1,
    recv_b1,
    send_b2,
    recv_b2,
    raw_ref,
    sum_own,
    sum_peer,
    text_sum,
    txp_out,
    txp_in,
    imp_out,
    imp_in,
    lossp_out,
    lossp_in,
    in_sem,
    out_sem,
    swap_send,
    swap_recv,
    z_send,
    z_recv,
    zid_send,
    zid_recv,
    x_send,
    x_recv,
):
    blk = lax.axis_index("blk")
    grp = lax.axis_index("group")
    col = blk % 2
    peer = {"blk": blk + 1 - 2 * col}
    up = {"blk": (blk + 2) % 16}
    down = {"blk": (blk + 14) % 16}
    y, u = grp // FAN, grp % FAN
    y_peer = [{"group": ((y + k) % FAN) * FAN + u} for k in range(FAN)]
    u_peer = [{"group": y * FAN + (u + k) % FAN} for k in range(FAN)]

    loads = [
        pltpu.make_async_copy(src, dst, in_sem.at[i])
        for i, (src, dst) in enumerate(
            [
                (images_hbm, images),
                (image_ids_hbm, image_ids_in),
                (lengths_hbm, meta.at[0]),
                (destination_hbm, meta.at[1]),
                (slot_hbm, meta.at[2]),
                (caption_ids_hbm, meta.at[3]),
                (tokens_hbm, tokens),
                (head_hbm, head),
            ]
        )
    ]
    for load in loads:
        load.start()

    barrier = pltpu.get_barrier_semaphore()
    greeted = [peer, up, down] + y_peer[1:] + u_peer[1:]
    for other in greeted:
        pl.semaphore_signal(barrier, inc=1, device_id=other, device_id_type=MESH)

    def remote(src, dst, send, recv, to):
        return pltpu.make_async_remote_copy(
            src_ref=src, dst_ref=dst, send_sem=send, recv_sem=recv, device_id=to, device_id_type=MESH
        )

    loads[0].wait()
    loads[1].wait()
    image_f = images[...].astype(F32)
    image_factor = lax.rsqrt(jnp.sum(image_f * image_f, axis=1, keepdims=True) + NORM_EPS)
    im_buf[0:ROWS, :] = (image_f * image_factor).astype(BF16)
    im_ids[0] = jnp.broadcast_to(image_ids_in[...].astype(F32), (8, ROWS))

    for i in range(2, 6):
        loads[i].wait()
    lengths = meta[0]
    position = meta[1] * 2 + meta[2]
    places = 288
    spread = iota((CAPS_HERE, places), 1) - iota((CAPS_HERE, places), 0)
    hit = spread == 0
    level = jnp.zeros((1, places), jnp.int32)
    lane = iota((1, places), 1)
    for step in range(1, TOKENS):
        hit = hit | (spread == CAPS_HERE * step)
        level = level + (lane >= CAPS_HERE * step).astype(jnp.int32)
    spread_b = hit.astype(F32).astype(BF16)
    wide_length = dot(jnp.broadcast_to(lengths, (16, CAPS_HERE)).astype(F32).astype(BF16), spread_b)[0:1, :]
    wide_position = dot(jnp.broadcast_to(position, (16, CAPS_HERE)).astype(F32).astype(BF16), spread_b)[0:1, :]
    wide_position = jnp.where(level.astype(F32) < wide_length, wide_position, -1.0)

    def row_slot(r):
        return ((y + (r >> 4)) % FAN) * 16 + ((u + ((r >> 1) & 7)) % FAN) * 2 + (r & 1)

    def gather_matrix(order):
        return (order.astype(F32) == wide_position).astype(F32).astype(BF16)

    def own_captions(order):
        return order == position

    loads[6].wait()
    order_a = row_slot(iota((ROWS, 1), 0))
    order_b = row_slot(swap_pairs(iota((ROWS, 1), 0)))
    here_a = own_captions(order_a)
    here_b = own_captions(order_b)
    count_a = jnp.sum(jnp.where(here_a, lengths, 0).astype(F32), axis=1, keepdims=True)
    count_b = jnp.sum(jnp.where(here_b, lengths, 0).astype(F32), axis=1, keepdims=True)
    ids_b = jnp.sum(jnp.where(here_b, meta[3] + 1, 0).astype(F32), axis=1, keepdims=True).astype(jnp.int32)
    send_a1[...] = (dot(gather_matrix(order_a), tokens[:, 0:HALF]) / jnp.maximum(count_a, 1.0)).astype(BF16)
    send_b1[:, 0 : D - HALF] = (
        dot(gather_matrix(order_b), tokens[:, HALF:D]) / jnp.maximum(count_b, 1.0)
    ).astype(BF16)
    id_lane = iota((ROWS, ROWS), 1)
    send_b1[:, D - HALF : HALF] = (
        jnp.where(id_lane == 0, ids_b >> 5, jnp.where(id_lane == 1, ids_b & 31, 0)).astype(F32).astype(BF16)
    )

    pl.semaphore_wait(barrier, len(greeted))

    def swap(stage, src, dst, to):
        copies = []
        for k in range(1, FAN):
            copy = remote(
                src.at[pl.ds(k * 16, 16)],
                dst.at[pl.ds(k * 16, 16)],
                swap_send.at[stage, k],
                swap_recv.at[stage, k],
                to[k],
            )
            copy.start()
            copies.append(copy)
        dst[0:16, :] = src[0:16, :]
        return copies

    def own_along_z(kind, buf, ids):
        copies = []
        for way, (to, place) in enumerate(((up, 1), (down, 2))):
            tag = zid_send.at[kind, place], zid_recv.at[kind, place]
            copies.append(remote(ids.at[0], ids.at[place], *tag, to))
        for piece in range(PIECES):
            for way, (to, place) in enumerate(((up, 1), (down, 2))):
                copies.append(
                    remote(
                        buf.at[pl.ds(piece * PIECE, PIECE)],
                        buf.at[pl.ds(place * ROWS + piece * PIECE, PIECE)],
                        z_send.at[kind, place, piece],
                        z_recv.at[kind, place, piece],
                        to,
                    )
                )
        for copy in copies:
            copy.start()
        return copies

    def pass_along_z(kind, buf, ids, arriving):
        copies = []
        for way, (to, place) in enumerate(((up, 1), (down, 2))):
            arriving[way].wait_recv()
            far = place + 2
            copy = remote(
                ids.at[place], ids.at[far], zid_send.at[kind, far], zid_recv.at[kind, far], to
            )
            copy.start()
            copies.append(copy)
        for piece in range(PIECES):
            for way, (to, place) in enumerate(((up, 1), (down, 2))):
                arriving[2 + piece * 2 + way].wait_recv()
                far = place + 2
                copy = remote(
                    buf.at[pl.ds(place * ROWS + piece * PIECE, PIECE)],
                    buf.at[pl.ds(far * ROWS + piece * PIECE, PIECE)],
                    z_send.at[kind, far, piece],
                    z_recv.at[kind, far, piece],
                    to,
                )
                copy.start()
                copies.append(copy)
        return copies

    def to_peer(i, src, dst):
        copy = remote(src, dst, x_send.at[i], x_recv.at[i], peer)
        copy.start()
        return copy

    sent = []
    swap_a1 = swap(0, send_a1, recv_a1, y_peer)
    swap_b1 = swap(1, send_b1, recv_b1, u_peer)
    im_near = own_along_z(0, im_buf, im_ids)
    im_x = [to_peer(0, im_buf.at[pl.ds(0, ROWS)], im_peer), to_peer(1, im_ids.at[0], im_peer_ids)]

    r_out = iota((ROWS, ROWS), 0)
    r_in = iota((ROWS, ROWS), 1)
    turn = (swap_pairs(r_out) == r_in).astype(F32).astype(BF16)
    for copy in swap_a1:
        copy.wait_recv()
    send_a2[...] = dot(turn, recv_a1[...]).astype(BF16)
    swap_a2 = swap(2, send_a2, recv_a2, u_peer)
    for copy in swap_b1:
        copy.wait_recv()
    send_b2[...] = dot(turn, recv_b1[...]).astype(BF16)
    swap_b2 = swap(3, send_b2, recv_b2, y_peer)

    im_far = pass_along_z(0, im_buf, im_ids, im_near)

    def home_slot(r):
        return ((y + FAN - (r >> 4)) % FAN) * 16 + ((u + FAN - ((r >> 1) & 7)) % FAN) * 2 + (r & 1)

    for copy in swap_a2:
        copy.wait_recv()
    home_a = (home_slot(swap_pairs(r_in)) == r_out).astype(F32).astype(BF16)
    pooled_a = dot(home_a, recv_a2[...]).astype(BF16)
    loads[7].wait()
    raw_a = dot(pooled_a, head[0:HALF, :])
    for copy in swap_b2:
        copy.wait_recv()
    home_b = (home_slot(r_in) == r_out).astype(F32).astype(BF16)
    pooled_b = dot(home_b, recv_b2[...]).astype(BF16)
    raw = raw_a + dot(pooled_b[:, 0 : D - HALF], head[HALF:D, :])
    raw_ref[...] = raw
    text_factor = lax.rsqrt(jnp.sum(raw * raw, axis=1, keepdims=True) + NORM_EPS)
    tx_buf[0:ROWS, :] = (raw * text_factor).astype(BF16)
    id_codes = pooled_b[:, D - HALF : HALF]
    weigh_in = jnp.where(r_in == 0, 32.0, jnp.where(r_in == 1, 1.0, 0.0)).astype(BF16)
    tx_cols = dot_t(weigh_in, id_codes) - 1.0
    tx_ids[0] = tx_cols[0:8, :]
    tx_near = own_along_z(1, tx_buf, tx_ids)
    tx_x = [to_peer(2, tx_buf.at[pl.ds(0, ROWS)], tx_peer), to_peer(3, tx_ids.at[0], tx_peer_ids)]

    scale = scale_ref[0]
    bias = bias_ref[0]

    def as_rows(ids):
        return jnp.transpose(jnp.broadcast_to(ids, (ROWS, ROWS)))

    def terms(rows, row_ids, cols, col_ids, text_is_rows, far_masks):
        logits = scale * dot_t(rows, cols) + bias
        blocks = len(col_ids)
        wide_cols = jnp.concatenate(col_ids, axis=1)
        wide_rows = jnp.concatenate([row_ids] * blocks, axis=1)
        same = wide_rows == wide_cols
        live = ((wide_rows if text_is_rows else wide_cols) >= 0.0).astype(F32)
        if far_masks is not None:
            ones = jnp.ones((1, ROWS), F32)
            allowed = jnp.concatenate(
                [ones] * (blocks - 2) + [ones * far_masks[0], ones * far_masks[1]], axis=1
            )
            live = live * allowed
        flipped = jnp.where(same, -logits, logits)
        small = jnp.exp(-jnp.abs(flipped))
        sigmoid = jnp.where(flipped >= 0.0, 1.0, small) / (1.0 + small)
        weights = (live * jnp.where(same, -scale, scale) * sigmoid).astype(BF16)
        if text_is_rows:
            return weights, None
        softplus = jnp.maximum(flipped, 0.0) + jnp.log1p(small)
        return weights, jnp.sum(live * softplus, axis=1, keepdims=True)

    col_f = col.astype(F32)
    far_masks = (col_f, 1.0 - col_f)

    for copy in im_far:
        copy.wait_recv()
    im_cols = [im_ids[place][0:1, :] for place in range(5)]
    weights, _ = terms(tx_buf[0:ROWS, :], as_rows(tx_cols[0:1, :]), im_buf[...], im_cols, True, None)
    text_sum[...] = dot(weights, im_buf[...])

    for copy in im_x:
        copy.wait_recv()
    own_rows = as_rows(im_ids[0][0:1, :])
    peer_rows = as_rows(im_peer_ids[0:1, :])

    tx_far = pass_along_z(1, tx_buf, tx_ids, tx_near)

    for copy in tx_x:
        copy.wait_recv()
    weights, _ = terms(tx_peer[...], as_rows(tx_peer_ids[0:1, :]), im_buf[...], im_cols, True, far_masks)
    txp_out[...] = dot(weights, im_buf[...]).astype(BF16)
    txp = to_peer(4, txp_out, txp_in)

    def image_terms(rows, row_ids, place, blocks, masks):
        cols = tx_buf[place * ROWS : (place + blocks) * ROWS, :]
        ids = [tx_ids[p][0:1, :] for p in range(place, place + blocks)]
        weights, loss = terms(rows, row_ids, cols, ids, False, masks)
        return dot(weights, cols), loss

    own_im = im_buf[0:ROWS, :]
    part, loss_own = image_terms(own_im, own_rows, 0, 3, None)
    sum_own[...] = part
    part, loss_peer = image_terms(im_peer[...], peer_rows, 0, 3, None)
    sum_peer[...] = part

    for copy in tx_far:
        copy.wait_recv()
    part, loss = image_terms(im_peer[...], peer_rows, 3, 2, far_masks)
    imp_out[...] = (sum_peer[...] + part).astype(BF16)
    loss_peer = loss_peer + loss
    lossp_out[...] = jnp.transpose(jnp.broadcast_to(loss_peer, (ROWS, ROWS)))[0:8, :]
    imp = [to_peer(5, imp_out, imp_in), to_peer(6, lossp_out, lossp_in)]
    part, loss = image_terms(own_im, own_rows, 3, 2, None)
    sum_own[...] += part
    loss_own = loss_own + loss
    loss_row = jnp.transpose(jnp.broadcast_to(loss_own, (ROWS, ROWS)))[0:1, :]

    txp.wait_recv()
    total = text_sum[...] + txp_in[...].astype(F32)
    text_norm = raw_ref[...] * text_factor
    along = jnp.sum(text_norm * total, axis=1, keepdims=True)
    text_raw_grad = (text_factor * (total - text_norm * along)).astype(BF16)
    out_text[...] = dot_t(text_raw_grad, head[...])
    store_text = pltpu.make_async_copy(out_text, text_grad_hbm, out_sem.at[0])
    store_text.start()

    for copy in imp:
        copy.wait_recv()
    out_loss[...] = loss_row + lossp_in[0:1, :]
    store_loss = pltpu.make_async_copy(out_loss, loss_hbm, out_sem.at[1])
    store_loss.start()
    total = sum_own[...] + imp_in[...].astype(F32)
    image_norm = images[...].astype(F32) * image_factor
    along = jnp.sum(image_norm * total, axis=1, keepdims=True)
    out_image[...] = image_factor * (total - image_norm * along)
    store_image = pltpu.make_async_copy(out_image, image_grad_hbm, out_sem.at[2])
    store_image.start()

    for copy in swap_a1 + swap_b1 + swap_a2 + swap_b2 + im_near + im_far + im_x + tx_near + tx_far + tx_x:
        copy.wait_send()
    for copy in [txp] + imp:
        copy.wait_send()
    store_text.wait()
    store_loss.wait()
    store_image.wait()


def per_device(
    tokens, lengths, caption_ids, destination, slot, images, image_ids, head_weight, logit_scale, logit_bias
):
    any_spec = pl.BlockSpec(memory_space=pl.ANY)
    smem_spec = pl.BlockSpec(memory_space=pltpu.SMEM)

    def vmem(shape, dtype):
        return pltpu.VMEM(shape, dtype)

    block = (ROWS, D)
    flat_tokens = jnp.transpose(tokens, (1, 0, 2)).reshape(TOKENS * CAPS_HERE, D)
    as_row = lambda a: a.reshape(1, a.shape[0])
    image_grad, text_grad, loss = pl.pallas_call(
        kernel,
        out_shape=(
            jax.ShapeDtypeStruct(block, F32),
            jax.ShapeDtypeStruct(block, F32),
            jax.ShapeDtypeStruct((1, ROWS), F32),
        ),
        in_specs=[any_spec] * 8 + [smem_spec] * 2,
        out_specs=(any_spec, any_spec, any_spec),
        scratch_shapes=[
            vmem((TOKENS * CAPS_HERE, D), BF16),
            vmem((4, 1, CAPS_HERE), jnp.int32),
            vmem(block, BF16),
            vmem((1, ROWS), jnp.int32),
            vmem((D, D), BF16),
            vmem(block, F32),
            vmem(block, F32),
            vmem((1, ROWS), F32),
            vmem((5 * ROWS, D), BF16),
            vmem((5, 8, ROWS), F32),
            vmem(block, BF16),
            vmem((8, ROWS), F32),
            vmem((5 * ROWS, D), BF16),
            vmem((5, 8, ROWS), F32),
            vmem(block, BF16),
            vmem((8, ROWS), F32),
        ]
        + [vmem((ROWS, HALF), BF16)] * 8
        + [
            vmem(block, F32),
            vmem(block, F32),
            vmem(block, F32),
            vmem(block, F32),
            vmem(block, BF16),
            vmem(block, BF16),
            vmem(block, BF16),
            vmem(block, BF16),
            vmem((8, ROWS), F32),
            vmem((8, ROWS), F32),
            pltpu.SemaphoreType.DMA((8,)),
            pltpu.SemaphoreType.DMA((3,)),
            pltpu.SemaphoreType.DMA((4, FAN)),
            pltpu.SemaphoreType.DMA((4, FAN)),
            pltpu.SemaphoreType.DMA((2, 5, PIECES)),
            pltpu.SemaphoreType.DMA((2, 5, PIECES)),
            pltpu.SemaphoreType.DMA((2, 5)),
            pltpu.SemaphoreType.DMA((2, 5)),
            pltpu.SemaphoreType.DMA((7,)),
            pltpu.SemaphoreType.DMA((7,)),
        ],
        compiler_params=pltpu.CompilerParams(
            collective_id=0, has_side_effects=True, vmem_limit_bytes=40 * 1024 * 1024
        ),
        name="band",
    )(
        flat_tokens,
        as_row(lengths),
        as_row(caption_ids),
        as_row(destination),
        as_row(slot),
        images,
        as_row(image_ids),
        head_weight,
        logit_scale,
        logit_bias,
    )
    return (image_grad, text_grad, loss.reshape(ROWS))


def solution(mesh):
    spec1 = P(("blk", "group"))
    spec2 = P(("blk", "group"), None)
    return jax.shard_map(
        per_device,
        mesh=mesh,
        in_specs=(
            P(("blk", "group"), None, None),
            spec1,
            spec1,
            spec1,
            spec1,
            spec2,
            spec1,
            P(None, None),
            P(None),
            P(None),
        ),
        out_specs=(spec2, spec2, spec1),
        check_vma=False,
    )
```

time: 236 us -> 78.8 us (0.33)
  the two profiles are of different devices: /device:TPU:6 before, /device:TPU:1 now
where the time goes in v1:
time: 78.8 us; the launch traced here: 78.5 us
  Pallas kernels  67.3 us (85%)
  local copies, waits for them, and re-layouts  9.21 us (12%)
  between operations  1.95 us (2%)
    pallas_call x1, Pallas kernels, per_device(): pl.pallas_call(kernel, out_shape=(jax.ShapeDtypeStruct(block, F32), jax.S...  67.3 us
    unnamed x19, local copies, waits for them, and re-layouts  9.21 us

profile of v1, /device:TPU:1, one launch (start us, length us, event | category | flops | bytes accessed | tf_op | source)
XLA Modules:
  0.0 78.5 jit_solution(8447846797994477609)
XLA Ops:
  1.9 0.0 copy-start
  1.9 1.7 %copy-done = bf16[1152,1152]{1,0:T(8,128)(2,1)S(1)} copy-done((bf16[1152,1152]{1,0:T(8,128)(2,1)S(1)}, bf16[1152,1152]{1,0:T(8,128)(2,1)}, u32[]{:S(2)}) %copy-start) | copy-done | bytes 2654232
  3.7 0.0 copy-start.1
  3.7 1.1 %copy-done.1 = bf16[48,6,1152]{2,0,1:T(8,128)(2,1)S(1)} copy-done((bf16[48,6,1152]{2,0,1:T(8,128)(2,1)S(1)}, bf16[48,6,1152]{2,0,1:T(8,128)(2,1)}, u32[]{:S(2)}) %copy-start.1) | copy-done | bytes 663576
  4.8 0.0 copy-start.2
  4.8 1.0 %copy-done.2 = bf16[128,1152]{1,0:T(8,128)(2,1)S(1)} copy-done((bf16[128,1152]{1,0:T(8,128)(2,1)S(1)}, bf16[128,1152]{1,0:T(8,128)(2,1)}, u32[]{:S(2)}) %copy-start.2) | copy-done | bytes 294936
  5.7 0.0 copy-start.3
  5.7 0.7 copy-done.3
  6.4 0.0 copy-start.4
  6.4 0.7 copy-done.4
  7.0 0.0 copy-start.5
  7.0 0.7 copy-done.5
  7.7 0.0 copy-start.6
  7.7 0.7 copy-done.6
  8.4 0.0 copy-start.7
  8.4 0.7 copy-done.7
  9.0 67.3 %band.1 = (f32[128,1152]{1,0:T(8,128)S(1)}, f32[128,1152]{1,0:T(8,128)S(1)}, f32[1,128]{1,0:T(1,128)S(1)}) custom-call(bf16[288,1152]{1,0:T(8,128)(2,1)S(1)} %bitcast.9, s32[1,48]{1,0:T(1,128)S(1)} %bitcast.10, s32[1,48]{1,0:T(1,128)S(1)} %bitcast.11, s32[1,48]{1,0:T(1,128)S(1)} %bitcast.12, s32[1,48]{1,0:T(1,128)S(1)} %bitcast.13, ...), custom_call_target="tpu_custom_call" | custom-call | tf_op jit(solution)/shard_map/band/pallas_call | solution.py:412
  76.3 0.8 %copy.18 = f32[128,1152]{1,0:T(8,128)} copy(f32[128,1152]{1,0:T(8,128)S(1)} %get-tuple-element.12) | data formatting | bytes 1179648
  77.1 0.8 %copy.19 = f32[128,1152]{1,0:T(8,128)} copy(f32[128,1152]{1,0:T(8,128)S(1)} %get-tuple-element.13) | data formatting | bytes 1179648
  78.0 0.5 copy.20
Async XLA Ops:
  1.9 1.8 %copy-start = (bf16[1152,1152]{1,0:T(8,128)(2,1)S(1)}, bf16[1152,1152]{1,0:T(8,128)(2,1)}, u32[]{:S(2)}) copy-start(bf16[1152,1152]{1,0:T(8,128)(2,1)} %head_hbm.1) | copy-start | bytes 7962628
  3.7 1.1 %copy-start.1 = (bf16[48,6,1152]{2,0,1:T(8,128)(2,1)S(1)}, bf16[48,6,1152]{2,0,1:T(8,128)(2,1)}, u32[]{:S(2)}) copy-start(bf16[48,6,1152]{2,0,1:T(8,128)(2,1)} %param.10) | copy-start | bytes 1990660
  4.8 1.0 %copy-start.2 = (bf16[128,1152]{1,0:T(8,128)(2,1)S(1)}, bf16[128,1152]{1,0:T(8,128)(2,1)}, u32[]{:S(2)}) copy-start(bf16[128,1152]{1,0:T(8,128)(2,1)} %images_hbm.1) | copy-start | bytes 884740
  5.7 0.7 copy-start.3
  6.4 0.7 copy-start.4
  7.0 0.7 copy-start.5
  7.7 0.7 copy-start.6
  8.4 0.7 copy-start.7

commit v2 on v1

--- a/solution.py
+++ b/solution.py
@@ -14,6 +14,8 @@
 FAN = 8
 PIECES = 2
 PIECE = ROWS // PIECES
+EARLY = 32
+HALF_ROWS = ROWS // 2
 MESH = pl.DeviceIdType.MESH
 BF16 = jnp.bfloat16
 F32 = jnp.float32
@@ -46,17 +48,14 @@
     head_hbm,
     scale_ref,
     bias_ref,
-    image_grad_hbm,
-    text_grad_hbm,
-    loss_hbm,
+    out_image,
+    out_text,
+    out_loss,
     tokens,
     meta,
     images,
     image_ids_in,
     head,
-    out_image,
-    out_text,
-    out_loss,
     im_buf,
     im_ids,
     im_peer,
@@ -84,7 +83,6 @@
     lossp_out,
     lossp_in,
     in_sem,
-    out_sem,
     swap_send,
     swap_recv,
     z_send,
@@ -253,7 +251,10 @@
     swap_a1 = swap(0, send_a1, recv_a1, y_peer)
     swap_b1 = swap(1, send_b1, recv_b1, u_peer)
     im_near = own_along_z(0, im_buf, im_ids)
-    im_x = [to_peer(0, im_buf.at[pl.ds(0, ROWS)], im_peer), to_peer(1, im_ids.at[0], im_peer_ids)]
+    im_x = [
+        to_peer(0, im_buf.at[pl.ds(0, EARLY)], im_peer.at[pl.ds(0, EARLY)]),
+        to_peer(1, im_ids.at[0], im_peer_ids),
+    ]
 
     r_out = iota((ROWS, ROWS), 0)
     r_in = iota((ROWS, ROWS), 1)
@@ -262,6 +263,7 @@
         copy.wait_recv()
     send_a2[...] = dot(turn, recv_a1[...]).astype(BF16)
     swap_a2 = swap(2, send_a2, recv_a2, u_peer)
+    im_x.append(to_peer(7, im_buf.at[pl.ds(EARLY, ROWS - EARLY)], im_peer.at[pl.ds(EARLY, ROWS - EARLY)]))
     for copy in swap_b1:
         copy.wait_recv()
     send_b2[...] = dot(turn, recv_b1[...]).astype(BF16)
@@ -361,7 +363,11 @@
     imp_out[...] = (sum_peer[...] + part).astype(BF16)
     loss_peer = loss_peer + loss
     lossp_out[...] = jnp.transpose(jnp.broadcast_to(loss_peer, (ROWS, ROWS)))[0:8, :]
-    imp = [to_peer(5, imp_out, imp_in), to_peer(6, lossp_out, lossp_in)]
+    imp = [
+        to_peer(6, lossp_out, lossp_in),
+        to_peer(5, imp_out.at[pl.ds(0, HALF_ROWS)], imp_in.at[pl.ds(0, HALF_ROWS)]),
+        to_peer(8, imp_out.at[pl.ds(HALF_ROWS, HALF_ROWS)], imp_in.at[pl.ds(HALF_ROWS, HALF_ROWS)]),
+    ]
     part, loss = image_terms(own_im, own_rows, 3, 2, None)
     sum_own[...] += part
     loss_own = loss_own + loss
@@ -373,34 +379,40 @@
     along = jnp.sum(text_norm * total, axis=1, keepdims=True)
     text_raw_grad = (text_factor * (total - text_norm * along)).astype(BF16)
     out_text[...] = dot_t(text_raw_grad, head[...])
-    store_text = pltpu.make_async_copy(out_text, text_grad_hbm, out_sem.at[0])
-    store_text.start()
-
-    for copy in imp:
-        copy.wait_recv()
+
+    imp[0].wait_recv()
     out_loss[...] = loss_row + lossp_in[0:1, :]
-    store_loss = pltpu.make_async_copy(out_loss, loss_hbm, out_sem.at[1])
-    store_loss.start()
-    total = sum_own[...] + imp_in[...].astype(F32)
-    image_norm = images[...].astype(F32) * image_factor
-    along = jnp.sum(image_norm * total, axis=1, keepdims=True)
-    out_image[...] = image_factor * (total - image_norm * along)
-    store_image = pltpu.make_async_copy(out_image, image_grad_hbm, out_sem.at[2])
-    store_image.start()
+    for half in range(2):
+        imp[1 + half].wait_recv()
+        top, end = half * HALF_ROWS, (half + 1) * HALF_ROWS
+        factor = image_factor[top:end, :]
+        total = sum_own[top:end, :] + imp_in[top:end, :].astype(F32)
+        image_norm = images[top:end, :].astype(F32) * factor
+        along = jnp.sum(image_norm * total, axis=1, keepdims=True)
+        out_image[top:end, :] = factor * (total - image_norm * along)
 
     for copy in swap_a1 + swap_b1 + swap_a2 + swap_b2 + im_near + im_far + im_x + tx_near + tx_far + tx_x:
         copy.wait_send()
     for copy in [txp] + imp:
         copy.wait_send()
-    store_text.wait()
-    store_loss.wait()
-    store_image.wait()
+
+
+def settle(image_in, text_in, loss_in, image_out, text_out, loss_out, sem):
+    copies = [
+        pltpu.make_async_copy(src, dst, sem.at[i])
+        for i, (src, dst) in enumerate(((image_in, image_out), (text_in, text_out), (loss_in, loss_out)))
+    ]
+    for copy in copies:
+        copy.start()
+    for copy in copies:
+        copy.wait()
 
 
 def per_device(
     tokens, lengths, caption_ids, destination, slot, images, image_ids, head_weight, logit_scale, logit_bias
 ):
     any_spec = pl.BlockSpec(memory_space=pl.ANY)
+    vmem_spec = pl.BlockSpec(memory_space=pltpu.VMEM)
     smem_spec = pl.BlockSpec(memory_space=pltpu.SMEM)
 
     def vmem(shape, dtype):
@@ -411,22 +423,15 @@
     as_row = lambda a: a.reshape(1, a.shape[0])
     image_grad, text_grad, loss = pl.pallas_call(
         kernel,
-        out_shape=(
-            jax.ShapeDtypeStruct(block, F32),
-            jax.ShapeDtypeStruct(block, F32),
-            jax.ShapeDtypeStruct((1, ROWS), F32),
-        ),
+        out_shape=(pltpu.VMEM(block, F32), pltpu.VMEM(block, F32), pltpu.VMEM((1, ROWS), F32)),
         in_specs=[any_spec] * 8 + [smem_spec] * 2,
-        out_specs=(any_spec, any_spec, any_spec),
+        out_specs=(vmem_spec,) * 3,
         scratch_shapes=[
             vmem((TOKENS * CAPS_HERE, D), BF16),
             vmem((4, 1, CAPS_HERE), jnp.int32),
             vmem(block, BF16),
             vmem((1, ROWS), jnp.int32),
             vmem((D, D), BF16),
-            vmem(block, F32),
-            vmem(block, F32),
-            vmem((1, ROWS), F32),
             vmem((5 * ROWS, D), BF16),
             vmem((5, 8, ROWS), F32),
             vmem(block, BF16),
@@ -449,32 +454,49 @@
             vmem((8, ROWS), F32),
             vmem((8, ROWS), F32),
             pltpu.SemaphoreType.DMA((8,)),
-            pltpu.SemaphoreType.DMA((3,)),
             pltpu.SemaphoreType.DMA((4, FAN)),
             pltpu.SemaphoreType.DMA((4, FAN)),
             pltpu.SemaphoreType.DMA((2, 5, PIECES)),
             pltpu.SemaphoreType.DMA((2, 5, PIECES)),
             pltpu.SemaphoreType.DMA((2, 5)),
             pltpu.SemaphoreType.DMA((2, 5)),
-            pltpu.SemaphoreType.DMA((7,)),
-            pltpu.SemaphoreType.DMA((7,)),
+            pltpu.SemaphoreType.DMA((9,)),
+            pltpu.SemaphoreType.DMA((9,)),
         ],
         compiler_params=pltpu.CompilerParams(
             collective_id=0, has_side_effects=True, vmem_limit_bytes=40 * 1024 * 1024
         ),
         name="band",
     )(
-        flat_tokens,
-        as_row(lengths),
-        as_row(caption_ids),
-        as_row(destination),
-        as_row(slot),
-        images,
-        as_row(image_ids),
-        head_weight,
+        *[
+            pltpu.with_memory_space_constraint(a, pltpu.HBM)
+            for a in (
+                flat_tokens,
+                as_row(lengths),
+                as_row(caption_ids),
+                as_row(destination),
+                as_row(slot),
+                images,
+                as_row(image_ids),
+                head_weight,
+            )
+        ],
         logit_scale,
         logit_bias,
     )
+    image_grad, text_grad, loss = pl.pallas_call(
+        settle,
+        out_shape=(
+            jax.ShapeDtypeStruct(block, F32),
+            jax.ShapeDtypeStruct(block, F32),
+            jax.ShapeDtypeStruct((1, ROWS), F32),
+        ),
+        in_specs=[vmem_spec] * 3,
+        out_specs=(any_spec, any_spec, any_spec),
+        scratch_shapes=[pltpu.SemaphoreType.DMA((3,))],
+        compiler_params=pltpu.CompilerParams(vmem_limit_bytes=40 * 1024 * 1024),
+        name="settle",
+    )(image_grad, text_grad, loss)
     return (image_grad, text_grad, loss.reshape(ROWS))
 
 

time: 78.8 us -> 66.4 us (0.84)
  local copies, waits for them, and re-layouts: 9.21 us -> 0 us
  Pallas kernels: 67.3 us -> 64.2 us
    unnamed x19 -> x0, local copies, waits for them, and re-layouts: 9.21 us -> none
    pallas_call x1 -> x2, Pallas kernels: 67.3 us -> 64.2 us  [the longest x1 63.1 us: per_device(): pl.pallas_call(kernel, out_shape=(pltpu.VMEM(block, F32), pltpu.VMEM(bloc...]
where the time goes in v2:
time: 66.4 us; the launch traced here: 66.1 us
  Pallas kernels  64.2 us (97%)
  between operations  1.93 us (3%)
    pallas_call x1, Pallas kernels, per_device(): pl.pallas_call(kernel, out_shape=(pltpu.VMEM(block, F32), pltpu.VMEM(bloc...  63.1 us

profile of v2, /device:TPU:1, one launch (start us, length us, event | category | flops | bytes accessed | tf_op | source)
XLA Modules:
  0.0 66.1 jit_solution(15280878294893808344)
XLA Ops:
  1.9 63.1 %band.1 = (f32[128,1152]{1,0:T(8,128)S(1)}, f32[128,1152]{1,0:T(8,128)S(1)}, f32[1,128]{1,0:T(1,128)S(1)}) custom-call(bf16[288,1152]{1,0:T(8,128)(2,1)} %bitcast.9, s32[1,48]{1,0:T(1,128)} %bitcast.10, s32[1,48]{1,0:T(1,128)} %bitcast.11, s32[1,48]{1,0:T(1,128)} %bitcast.12, s32[1,48]{1,0:T(1,128)} %bitcast.13, bf16[128,1152]{1,0:T(8,128)(2,1)} %images_hbm.1, ...), custom_call_target="tpu_custom_call" | custom-call | tf_op jit(solution)/shard_map/band/pallas_call | solution.py:424
  65.1 1.0 %settle.1 = (f32[128,1152]{1,0:T(8,128)}, f32[128,1152]{1,0:T(8,128)}, f32[1,128]{1,0:T(1,128)}) custom-call(f32[128,1152]{1,0:T(8,128)S(1)} %get-tuple-element.9.image_in, f32[128,1152]{1,0:T(8,128)S(1)} %get-tuple-element.10.text_in, f32[1,128]{1,0:T(1,128)S(1)} %get-tuple-element.11.loss_in), custom_call_target="tpu_custom_call" | custom-call | tf_op jit(solution)/shard_map/settle/pallas_call | solution.py:487

commit v3 on v2

--- a/solution.py
+++ b/solution.py
@@ -14,8 +14,8 @@
 FAN = 8
 PIECES = 2
 PIECE = ROWS // PIECES
-EARLY = 32
-HALF_ROWS = ROWS // 2
+PEER, CROSS, FAR = 5, 5, 8
+FAR_FIRST = (4, 3, 5, 2, 6, 1, 7)
 MESH = pl.DeviceIdType.MESH
 BF16 = jnp.bfloat16
 F32 = jnp.float32
@@ -58,12 +58,8 @@
     head,
     im_buf,
     im_ids,
-    im_peer,
-    im_peer_ids,
     tx_buf,
     tx_ids,
-    tx_peer,
-    tx_peer_ids,
     send_a1,
     recv_a1,
     send_a2,
@@ -73,15 +69,10 @@
     send_b2,
     recv_b2,
     raw_ref,
-    sum_own,
-    sum_peer,
+    image_sum,
     text_sum,
     txp_out,
     txp_in,
-    imp_out,
-    imp_in,
-    lossp_out,
-    lossp_in,
     in_sem,
     swap_send,
     swap_recv,
@@ -106,38 +97,33 @@
         pltpu.make_async_copy(src, dst, in_sem.at[i])
         for i, (src, dst) in enumerate(
             [
-                (images_hbm, images),
-                (image_ids_hbm, image_ids_in),
                 (lengths_hbm, meta.at[0]),
                 (destination_hbm, meta.at[1]),
                 (slot_hbm, meta.at[2]),
                 (caption_ids_hbm, meta.at[3]),
                 (tokens_hbm, tokens),
+                (images_hbm, images),
+                (image_ids_hbm, image_ids_in),
                 (head_hbm, head),
             ]
         )
     ]
-    for load in loads:
+    for load in loads[:5]:
         load.start()
 
     barrier = pltpu.get_barrier_semaphore()
     greeted = [peer, up, down] + y_peer[1:] + u_peer[1:]
     for other in greeted:
         pl.semaphore_signal(barrier, inc=1, device_id=other, device_id_type=MESH)
+    for load in loads[5:7]:
+        load.start()
 
     def remote(src, dst, send, recv, to):
         return pltpu.make_async_remote_copy(
             src_ref=src, dst_ref=dst, send_sem=send, recv_sem=recv, device_id=to, device_id_type=MESH
         )
 
-    loads[0].wait()
-    loads[1].wait()
-    image_f = images[...].astype(F32)
-    image_factor = lax.rsqrt(jnp.sum(image_f * image_f, axis=1, keepdims=True) + NORM_EPS)
-    im_buf[0:ROWS, :] = (image_f * image_factor).astype(BF16)
-    im_ids[0] = jnp.broadcast_to(image_ids_in[...].astype(F32), (8, ROWS))
-
-    for i in range(2, 6):
+    for i in range(4):
         loads[i].wait()
     lengths = meta[0]
     position = meta[1] * 2 + meta[2]
@@ -163,7 +149,8 @@
     def own_captions(order):
         return order == position
 
-    loads[6].wait()
+    loads[4].wait()
+    loads[7].start()
     order_a = row_slot(iota((ROWS, 1), 0))
     order_b = row_slot(swap_pairs(iota((ROWS, 1), 0)))
     here_a = own_captions(order_a)
@@ -182,64 +169,79 @@
 
     pl.semaphore_wait(barrier, len(greeted))
 
-    def swap(stage, src, dst, to):
+    def swap(stages):
+        copies = [[] for _ in stages]
+        for k in FAR_FIRST:
+            for i, (stage, src, dst, to) in enumerate(stages):
+                copy = remote(
+                    src.at[pl.ds(k * 16, 16)],
+                    dst.at[pl.ds(k * 16, 16)],
+                    swap_send.at[stage, k],
+                    swap_recv.at[stage, k],
+                    to[k],
+                )
+                copy.start()
+                copies[i].append(copy)
+        for stage, src, dst, to in stages:
+            dst[0:16, :] = src[0:16, :]
+        return copies
+
+    ways = ((up, 1), (down, 2))
+
+    def start_piece(kind, buf, piece, start=0, land=0):
         copies = []
-        for k in range(1, FAN):
+        for to, place in ways:
             copy = remote(
-                src.at[pl.ds(k * 16, 16)],
-                dst.at[pl.ds(k * 16, 16)],
-                swap_send.at[stage, k],
-                swap_recv.at[stage, k],
-                to[k],
+                buf.at[pl.ds(start * ROWS + piece * PIECE, PIECE)],
+                buf.at[pl.ds((land + place) * ROWS + piece * PIECE, PIECE)],
+                z_send.at[kind, place, piece],
+                z_recv.at[kind, place, piece],
+                to,
             )
             copy.start()
             copies.append(copy)
-        dst[0:16, :] = src[0:16, :]
         return copies
 
-    def own_along_z(kind, buf, ids):
+    def start_ids(kind, ids, start=0, land=0):
         copies = []
-        for way, (to, place) in enumerate(((up, 1), (down, 2))):
-            tag = zid_send.at[kind, place], zid_recv.at[kind, place]
-            copies.append(remote(ids.at[0], ids.at[place], *tag, to))
-        for piece in range(PIECES):
-            for way, (to, place) in enumerate(((up, 1), (down, 2))):
-                copies.append(
-                    remote(
-                        buf.at[pl.ds(piece * PIECE, PIECE)],
-                        buf.at[pl.ds(place * ROWS + piece * PIECE, PIECE)],
-                        z_send.at[kind, place, piece],
-                        z_recv.at[kind, place, piece],
-                        to,
-                    )
-                )
-        for copy in copies:
-            copy.start()
-        return copies
-
-    def pass_along_z(kind, buf, ids, arriving):
-        copies = []
-        for way, (to, place) in enumerate(((up, 1), (down, 2))):
-            arriving[way].wait_recv()
-            far = place + 2
+        for to, place in ways:
             copy = remote(
-                ids.at[place], ids.at[far], zid_send.at[kind, far], zid_recv.at[kind, far], to
+                ids.at[start], ids.at[land + place], zid_send.at[kind, place], zid_recv.at[kind, place], to
             )
             copy.start()
             copies.append(copy)
+        return copies
+
+    def own_along_z(kind, buf, ids):
+        copies = []
         for piece in range(PIECES):
-            for way, (to, place) in enumerate(((up, 1), (down, 2))):
-                arriving[2 + piece * 2 + way].wait_recv()
-                far = place + 2
-                copy = remote(
-                    buf.at[pl.ds(place * ROWS + piece * PIECE, PIECE)],
-                    buf.at[pl.ds(far * ROWS + piece * PIECE, PIECE)],
-                    z_send.at[kind, far, piece],
-                    z_recv.at[kind, far, piece],
-                    to,
-                )
-                copy.start()
-                copies.append(copy)
+            copies += start_piece(kind, buf, piece)
+        return copies + start_ids(kind, ids)
+
+    def pass_piece(kind, buf, arriving, piece):
+        copies = []
+        for way, (to, place) in enumerate(ways):
+            arriving[piece * 2 + way].wait_recv()
+            far = place + 2
+            copy = remote(
+                buf.at[pl.ds(place * ROWS + piece * PIECE, PIECE)],
+                buf.at[pl.ds(far * ROWS + piece * PIECE, PIECE)],
+                z_send.at[kind, far, piece],
+                z_recv.at[kind, far, piece],
+                to,
+            )
+            copy.start()
+            copies.append(copy)
+        return copies
+
+    def pass_ids(kind, ids, arriving):
+        copies = []
+        for way, (to, place) in enumerate(ways):
+            arriving[PIECES * 2 + way].wait_recv()
+            far = place + 2
+            copy = remote(ids.at[place], ids.at[far], zid_send.at[kind, far], zid_recv.at[kind, far], to)
+            copy.start()
+            copies.append(copy)
         return copies
 
     def to_peer(i, src, dst):
@@ -247,14 +249,15 @@
         copy.start()
         return copy
 
-    sent = []
-    swap_a1 = swap(0, send_a1, recv_a1, y_peer)
-    swap_b1 = swap(1, send_b1, recv_b1, u_peer)
+    swap_a1, swap_b1 = swap([(0, send_a1, recv_a1, y_peer), (1, send_b1, recv_b1, u_peer)])
+
+    loads[5].wait()
+    loads[6].wait()
+    image_f = images[...].astype(F32)
+    image_factor = lax.rsqrt(jnp.sum(image_f * image_f, axis=1, keepdims=True) + NORM_EPS)
+    im_buf[0:ROWS, :] = (image_f * image_factor).astype(BF16)
+    im_ids[0] = jnp.broadcast_to(image_ids_in[...].astype(F32), (8, ROWS))
     im_near = own_along_z(0, im_buf, im_ids)
-    im_x = [
-        to_peer(0, im_buf.at[pl.ds(0, EARLY)], im_peer.at[pl.ds(0, EARLY)]),
-        to_peer(1, im_ids.at[0], im_peer_ids),
-    ]
 
     r_out = iota((ROWS, ROWS), 0)
     r_in = iota((ROWS, ROWS), 1)
@@ -262,38 +265,46 @@
     for copy in swap_a1:
         copy.wait_recv()
     send_a2[...] = dot(turn, recv_a1[...]).astype(BF16)
-    swap_a2 = swap(2, send_a2, recv_a2, u_peer)
-    im_x.append(to_peer(7, im_buf.at[pl.ds(EARLY, ROWS - EARLY)], im_peer.at[pl.ds(EARLY, ROWS - EARLY)]))
+    (swap_a2,) = swap([(2, send_a2, recv_a2, u_peer)])
     for copy in swap_b1:
         copy.wait_recv()
     send_b2[...] = dot(turn, recv_b1[...]).astype(BF16)
-    swap_b2 = swap(3, send_b2, recv_b2, y_peer)
-
-    im_far = pass_along_z(0, im_buf, im_ids, im_near)
+    (swap_b2,) = swap([(3, send_b2, recv_b2, y_peer)])
+
+    im_far = []
+    for piece in range(PIECES):
+        im_far += pass_piece(0, im_buf, im_near, piece)
+    im_far += pass_ids(0, im_ids, im_near)
 
     def home_slot(r):
         return ((y + FAN - (r >> 4)) % FAN) * 16 + ((u + FAN - ((r >> 1) & 7)) % FAN) * 2 + (r & 1)
 
+    home_a = (home_slot(swap_pairs(r_in)) == r_out).astype(F32).astype(BF16)
+    home_b = (home_slot(r_in) == r_out).astype(F32).astype(BF16)
     for copy in swap_a2:
         copy.wait_recv()
-    home_a = (home_slot(swap_pairs(r_in)) == r_out).astype(F32).astype(BF16)
     pooled_a = dot(home_a, recv_a2[...]).astype(BF16)
     loads[7].wait()
     raw_a = dot(pooled_a, head[0:HALF, :])
     for copy in swap_b2:
         copy.wait_recv()
-    home_b = (home_slot(r_in) == r_out).astype(F32).astype(BF16)
     pooled_b = dot(home_b, recv_b2[...]).astype(BF16)
     raw = raw_a + dot(pooled_b[:, 0 : D - HALF], head[HALF:D, :])
-    raw_ref[...] = raw
     text_factor = lax.rsqrt(jnp.sum(raw * raw, axis=1, keepdims=True) + NORM_EPS)
-    tx_buf[0:ROWS, :] = (raw * text_factor).astype(BF16)
+    tx_near, tx_x = [], []
+    for piece in range(PIECES):
+        rows = pl.ds(piece * PIECE, PIECE)
+        top, end = piece * PIECE, (piece + 1) * PIECE
+        tx_buf[rows, :] = (raw[top:end, :] * text_factor[top:end, :]).astype(BF16)
+        tx_near += start_piece(1, tx_buf, piece)
+        tx_x.append(to_peer(piece, tx_buf.at[rows], tx_buf.at[pl.ds(PEER * ROWS + piece * PIECE, PIECE)]))
     id_codes = pooled_b[:, D - HALF : HALF]
     weigh_in = jnp.where(r_in == 0, 32.0, jnp.where(r_in == 1, 1.0, 0.0)).astype(BF16)
     tx_cols = dot_t(weigh_in, id_codes) - 1.0
     tx_ids[0] = tx_cols[0:8, :]
-    tx_near = own_along_z(1, tx_buf, tx_ids)
-    tx_x = [to_peer(2, tx_buf.at[pl.ds(0, ROWS)], tx_peer), to_peer(3, tx_ids.at[0], tx_peer_ids)]
+    tx_near += start_ids(1, tx_ids)
+    tx_x.append(to_peer(2, tx_ids.at[0], tx_ids.at[PEER]))
+    raw_ref[...] = raw
 
     scale = scale_ref[0]
     bias = bias_ref[0]
@@ -331,69 +342,78 @@
     im_cols = [im_ids[place][0:1, :] for place in range(5)]
     weights, _ = terms(tx_buf[0:ROWS, :], as_rows(tx_cols[0:1, :]), im_buf[...], im_cols, True, None)
     text_sum[...] = dot(weights, im_buf[...])
-
-    for copy in im_x:
-        copy.wait_recv()
-    own_rows = as_rows(im_ids[0][0:1, :])
-    peer_rows = as_rows(im_peer_ids[0:1, :])
-
-    tx_far = pass_along_z(1, tx_buf, tx_ids, tx_near)
-
-    for copy in tx_x:
-        copy.wait_recv()
-    weights, _ = terms(tx_peer[...], as_rows(tx_peer_ids[0:1, :]), im_buf[...], im_cols, True, far_masks)
-    txp_out[...] = dot(weights, im_buf[...]).astype(BF16)
-    txp = to_peer(4, txp_out, txp_in)
-
-    def image_terms(rows, row_ids, place, blocks, masks):
+    im_rows = as_rows(im_ids[0][0:1, :])
+
+    tx_far, tx_cross, txp = [], [], []
+    for piece in range(PIECES):
+        tx_far += pass_piece(1, tx_buf, tx_near, piece)
+        tx_x[piece].wait_recv()
+        if piece == 0:
+            tx_x[PIECES].wait_recv()
+            peer_rows = as_rows(tx_ids[PEER][0:1, :])
+        if piece == PIECES - 1:
+            tx_far += pass_ids(1, tx_ids, tx_near)
+            for part in range(PIECES):
+                tx_cross += start_piece(2, tx_buf, part, PEER, CROSS)
+            tx_cross += start_ids(2, tx_ids, PEER, CROSS)
+        top, end = piece * PIECE, (piece + 1) * PIECE
+        peer_text = tx_buf[PEER * ROWS + top : PEER * ROWS + end, :]
+        weights, _ = terms(peer_text, peer_rows[top:end, :], im_buf[...], im_cols, True, far_masks)
+        txp_out[top:end, :] = dot(weights, im_buf[...]).astype(BF16)
+        txp.append(to_peer(3 + piece, txp_out.at[pl.ds(top, PIECE)], txp_in.at[pl.ds(top, PIECE)]))
+
+    def image_terms(place, blocks):
         cols = tx_buf[place * ROWS : (place + blocks) * ROWS, :]
         ids = [tx_ids[p][0:1, :] for p in range(place, place + blocks)]
-        weights, loss = terms(rows, row_ids, cols, ids, False, masks)
+        weights, loss = terms(im_buf[0:ROWS, :], im_rows, cols, ids, False, None)
         return dot(weights, cols), loss
 
-    own_im = im_buf[0:ROWS, :]
-    part, loss_own = image_terms(own_im, own_rows, 0, 3, None)
-    sum_own[...] = part
-    part, loss_peer = image_terms(im_peer[...], peer_rows, 0, 3, None)
-    sum_peer[...] = part
-
-    for copy in tx_far:
-        copy.wait_recv()
-    part, loss = image_terms(im_peer[...], peer_rows, 3, 2, far_masks)
-    imp_out[...] = (sum_peer[...] + part).astype(BF16)
-    loss_peer = loss_peer + loss
-    lossp_out[...] = jnp.transpose(jnp.broadcast_to(loss_peer, (ROWS, ROWS)))[0:8, :]
-    imp = [
-        to_peer(6, lossp_out, lossp_in),
-        to_peer(5, imp_out.at[pl.ds(0, HALF_ROWS)], imp_in.at[pl.ds(0, HALF_ROWS)]),
-        to_peer(8, imp_out.at[pl.ds(HALF_ROWS, HALF_ROWS)], imp_in.at[pl.ds(HALF_ROWS, HALF_ROWS)]),
-    ]
-    part, loss = image_terms(own_im, own_rows, 3, 2, None)
-    sum_own[...] += part
+    part, loss_own = image_terms(0, 3)
+    image_sum[...] = part
+    part, loss = image_terms(PEER, 1)
+    image_sum[...] += part
     loss_own = loss_own + loss
-    loss_row = jnp.transpose(jnp.broadcast_to(loss_own, (ROWS, ROWS)))[0:1, :]
-
-    txp.wait_recv()
+
+    lacking = 4 - col
+    tx_last = []
+    for piece in range(PIECES):
+        for way in range(2):
+            tx_far[piece * 2 + way].wait_recv()
+        tx_last.append(
+            to_peer(
+                5 + piece,
+                tx_buf.at[pl.ds(pl.multiple_of(lacking * ROWS + piece * PIECE, PIECE), PIECE)],
+                tx_buf.at[pl.ds(FAR * ROWS + piece * PIECE, PIECE)],
+            )
+        )
+    for way in range(2):
+        tx_far[PIECES * 2 + way].wait_recv()
+    tx_last.append(to_peer(7, tx_ids.at[lacking], tx_ids.at[FAR]))
+    part, loss = image_terms(3, 2)
+    image_sum[...] += part
+    loss_own = loss_own + loss
+
+    for copy in txp:
+        copy.wait_recv()
     total = text_sum[...] + txp_in[...].astype(F32)
     text_norm = raw_ref[...] * text_factor
     along = jnp.sum(text_norm * total, axis=1, keepdims=True)
     text_raw_grad = (text_factor * (total - text_norm * along)).astype(BF16)
     out_text[...] = dot_t(text_raw_grad, head[...])
 
-    imp[0].wait_recv()
-    out_loss[...] = loss_row + lossp_in[0:1, :]
-    for half in range(2):
-        imp[1 + half].wait_recv()
-        top, end = half * HALF_ROWS, (half + 1) * HALF_ROWS
-        factor = image_factor[top:end, :]
-        total = sum_own[top:end, :] + imp_in[top:end, :].astype(F32)
-        image_norm = images[top:end, :].astype(F32) * factor
-        along = jnp.sum(image_norm * total, axis=1, keepdims=True)
-        out_image[top:end, :] = factor * (total - image_norm * along)
-
-    for copy in swap_a1 + swap_b1 + swap_a2 + swap_b2 + im_near + im_far + im_x + tx_near + tx_far + tx_x:
+    for copy in tx_cross + tx_last:
+        copy.wait_recv()
+    part, loss = image_terms(CROSS + 1, 3)
+    loss_own = loss_own + loss
+    total = image_sum[...] + part
+    image_norm = images[...].astype(F32) * image_factor
+    along = jnp.sum(image_norm * total, axis=1, keepdims=True)
+    out_image[...] = image_factor * (total - image_norm * along)
+    out_loss[...] = jnp.transpose(jnp.broadcast_to(loss_own, (ROWS, ROWS)))[0:1, :]
+
+    for copy in swap_a1 + swap_b1 + swap_a2 + swap_b2 + im_near + im_far:
         copy.wait_send()
-    for copy in [txp] + imp:
+    for copy in tx_near + tx_far + tx_x + tx_cross + txp + tx_last:
         copy.wait_send()
 
 
@@ -434,34 +454,25 @@
             vmem((D, D), BF16),
             vmem((5 * ROWS, D), BF16),
             vmem((5, 8, ROWS), F32),
-            vmem(block, BF16),
-            vmem((8, ROWS), F32),
-            vmem((5 * ROWS, D), BF16),
-            vmem((5, 8, ROWS), F32),
-            vmem(block, BF16),
-            vmem((8, ROWS), F32),
+            vmem((9 * ROWS, D), BF16),
+            vmem((9, 8, ROWS), F32),
         ]
         + [vmem((ROWS, HALF), BF16)] * 8
         + [
             vmem(block, F32),
             vmem(block, F32),
             vmem(block, F32),
-            vmem(block, F32),
             vmem(block, BF16),
             vmem(block, BF16),
-            vmem(block, BF16),
-            vmem(block, BF16),
-            vmem((8, ROWS), F32),
-            vmem((8, ROWS), F32),
             pltpu.SemaphoreType.DMA((8,)),
             pltpu.SemaphoreType.DMA((4, FAN)),
             pltpu.SemaphoreType.DMA((4, FAN)),
-            pltpu.SemaphoreType.DMA((2, 5, PIECES)),
-            pltpu.SemaphoreType.DMA((2, 5, PIECES)),
-            pltpu.SemaphoreType.DMA((2, 5)),
-            pltpu.SemaphoreType.DMA((2, 5)),
-            pltpu.SemaphoreType.DMA((9,)),
-            pltpu.SemaphoreType.DMA((9,)),
+            pltpu.SemaphoreType.DMA((3, 5, PIECES)),
+            pltpu.SemaphoreType.DMA((3, 5, PIECES)),
+            pltpu.SemaphoreType.DMA((3, 5)),
+            pltpu.SemaphoreType.DMA((3, 5)),
+            pltpu.SemaphoreType.DMA((8,)),
+            pltpu.SemaphoreType.DMA((8,)),
         ],
         compiler_params=pltpu.CompilerParams(
             collective_id=0, has_side_effects=True, vmem_limit_bytes=40 * 1024 * 1024

time: 66.4 us -> 64.5 us (0.971)
  Pallas kernels: 64.2 us -> 62.4 us
    pallas_call x1, Pallas kernels: 63.1 us -> 61.3 us  [per_device(): pl.pallas_call(kernel, out_shape=(pltpu.VMEM(block, F32), pltpu.VMEM(bloc...]
where the time goes in v3:
time: 64.5 us; the launch traced here: 64.3 us
  Pallas kernels  62.4 us (97%)
  between operations  1.93 us (3%)
    pallas_call x1, Pallas kernels, per_device(): pl.pallas_call(kernel, out_shape=(pltpu.VMEM(block, F32), pltpu.VMEM(bloc...  61.3 us

profile of v3, /device:TPU:1, one launch (start us, length us, event | category | flops | bytes accessed | tf_op | source)
XLA Modules:
  0.0 64.3 jit_solution(2833068169867743461)
XLA Ops:
  1.9 61.3 %band.1 = (f32[128,1152]{1,0:T(8,128)S(1)}, f32[128,1152]{1,0:T(8,128)S(1)}, f32[1,128]{1,0:T(1,128)S(1)}) custom-call(bf16[288,1152]{1,0:T(8,128)(2,1)} %bitcast.9, s32[1,48]{1,0:T(1,128)} %bitcast.10, s32[1,48]{1,0:T(1,128)} %bitcast.11, s32[1,48]{1,0:T(1,128)} %bitcast.12, s32[1,48]{1,0:T(1,128)} %bitcast.13, bf16[128,1152]{1,0:T(8,128)(2,1)} %images_hbm.1, ...), custom_call_target="tpu_custom_call" | custom-call | tf_op jit(solution)/shard_map/band/pallas_call | solution.py:444
  63.3 1.0 %settle.1 = (f32[128,1152]{1,0:T(8,128)}, f32[128,1152]{1,0:T(8,128)}, f32[1,128]{1,0:T(1,128)}) custom-call(f32[128,1152]{1,0:T(8,128)S(1)} %get-tuple-element.9.image_in, f32[128,1152]{1,0:T(8,128)S(1)} %get-tuple-element.10.text_in, f32[1,128]{1,0:T(1,128)S(1)} %get-tuple-element.11.loss_in), custom_call_target="tpu_custom_call" | custom-call | tf_op jit(solution)/shard_map/settle/pallas_call | solution.py:498

commit v4 on v3

--- a/solution.py
+++ b/solution.py
@@ -170,21 +170,16 @@
     pl.semaphore_wait(barrier, len(greeted))
 
     def swap(stages):
-        copies = [[] for _ in stages]
         for k in FAR_FIRST:
-            for i, (stage, src, dst, to) in enumerate(stages):
-                copy = remote(
-                    src.at[pl.ds(k * 16, 16)],
-                    dst.at[pl.ds(k * 16, 16)],
-                    swap_send.at[stage, k],
-                    swap_recv.at[stage, k],
-                    to[k],
-                )
-                copy.start()
-                copies[i].append(copy)
+            for stage, src, dst, to in stages:
+                rows = pl.ds(k * 16, 16)
+                remote(src.at[rows], dst.at[rows], swap_send.at[stage], swap_recv.at[stage], to[k]).start()
+        alls = []
         for stage, src, dst, to in stages:
             dst[0:16, :] = src[0:16, :]
-        return copies
+            rows = pl.ds(16, ROWS - 16)
+            alls.append([remote(src.at[rows], dst.at[rows], swap_send.at[stage], swap_recv.at[stage], to[1])])
+        return alls
 
     ways = ((up, 1), (down, 2))
 
@@ -279,17 +274,15 @@
     def home_slot(r):
         return ((y + FAN - (r >> 4)) % FAN) * 16 + ((u + FAN - ((r >> 1) & 7)) % FAN) * 2 + (r & 1)
 
-    home_a = (home_slot(swap_pairs(r_in)) == r_out).astype(F32).astype(BF16)
-    home_b = (home_slot(r_in) == r_out).astype(F32).astype(BF16)
+    home = (home_slot(r_in) == r_out).astype(F32).astype(BF16)
     for copy in swap_a2:
         copy.wait_recv()
-    pooled_a = dot(home_a, recv_a2[...]).astype(BF16)
+    pooled_a = dot(turn, recv_a2[...]).astype(BF16)
     loads[7].wait()
     raw_a = dot(pooled_a, head[0:HALF, :])
     for copy in swap_b2:
         copy.wait_recv()
-    pooled_b = dot(home_b, recv_b2[...]).astype(BF16)
-    raw = raw_a + dot(pooled_b[:, 0 : D - HALF], head[HALF:D, :])
+    raw = raw_a + dot(recv_b2[:, 0 : D - HALF], head[HALF:D, :])
     text_factor = lax.rsqrt(jnp.sum(raw * raw, axis=1, keepdims=True) + NORM_EPS)
     tx_near, tx_x = [], []
     for piece in range(PIECES):
@@ -298,7 +291,7 @@
         tx_buf[rows, :] = (raw[top:end, :] * text_factor[top:end, :]).astype(BF16)
         tx_near += start_piece(1, tx_buf, piece)
         tx_x.append(to_peer(piece, tx_buf.at[rows], tx_buf.at[pl.ds(PEER * ROWS + piece * PIECE, PIECE)]))
-    id_codes = pooled_b[:, D - HALF : HALF]
+    id_codes = recv_b2[:, D - HALF : HALF]
     weigh_in = jnp.where(r_in == 0, 32.0, jnp.where(r_in == 1, 1.0, 0.0)).astype(BF16)
     tx_cols = dot_t(weigh_in, id_codes) - 1.0
     tx_ids[0] = tx_cols[0:8, :]
@@ -399,7 +392,12 @@
     text_norm = raw_ref[...] * text_factor
     along = jnp.sum(text_norm * total, axis=1, keepdims=True)
     text_raw_grad = (text_factor * (total - text_norm * along)).astype(BF16)
-    out_text[...] = dot_t(text_raw_grad, head[...])
+    out_text[...] = dot_t(dot(home, text_raw_grad).astype(BF16), head[...])
+
+    for copy in swap_a1 + swap_b1 + swap_a2 + swap_b2 + im_near + im_far:
+        copy.wait_send()
+    for copy in tx_near + tx_x + txp + tx_far + tx_cross + tx_last:
+        copy.wait_send()
 
     for copy in tx_cross + tx_last:
         copy.wait_recv()
@@ -410,11 +408,6 @@
     along = jnp.sum(image_norm * total, axis=1, keepdims=True)
     out_image[...] = image_factor * (total - image_norm * along)
     out_loss[...] = jnp.transpose(jnp.broadcast_to(loss_own, (ROWS, ROWS)))[0:1, :]
-
-    for copy in swap_a1 + swap_b1 + swap_a2 + swap_b2 + im_near + im_far:
-        copy.wait_send()
-    for copy in tx_near + tx_far + tx_x + tx_cross + txp + tx_last:
-        copy.wait_send()
 
 
 def settle(image_in, text_in, loss_in, image_out, text_out, loss_out, sem):
@@ -465,8 +458,8 @@
             vmem(block, BF16),
             vmem(block, BF16),
             pltpu.SemaphoreType.DMA((8,)),
-            pltpu.SemaphoreType.DMA((4, FAN)),
-            pltpu.SemaphoreType.DMA((4, FAN)),
+            pltpu.SemaphoreType.DMA((4,)),
+            pltpu.SemaphoreType.DMA((4,)),
             pltpu.SemaphoreType.DMA((3, 5, PIECES)),
             pltpu.SemaphoreType.DMA((3, 5, PIECES)),
             pltpu.SemaphoreType.DMA((3, 5)),

time: 64.5 us -> 63.9 us (level)
  no operation moved by 1% of the time
where the time goes in v4:
time: 63.9 us; the launch traced here: 63.7 us
  Pallas kernels  61.8 us (97%)
  between operations  1.93 us (3%)
    pallas_call x1, Pallas kernels, per_device(): pl.pallas_call(kernel, out_shape=(pltpu.VMEM(block, F32), pltpu.VMEM(bloc...  60.7 us

profile of v4, /device:TPU:1, one launch (start us, length us, event | category | flops | bytes accessed | tf_op | source)
XLA Modules:
  0.0 63.7 jit_solution(1680891435120213084)
XLA Ops:
  1.9 60.7 %band.1 = (f32[128,1152]{1,0:T(8,128)S(1)}, f32[128,1152]{1,0:T(8,128)S(1)}, f32[1,128]{1,0:T(1,128)S(1)}) custom-call(bf16[288,1152]{1,0:T(8,128)(2,1)} %bitcast.9, s32[1,48]{1,0:T(1,128)} %bitcast.10, s32[1,48]{1,0:T(1,128)} %bitcast.11, s32[1,48]{1,0:T(1,128)} %bitcast.12, s32[1,48]{1,0:T(1,128)} %bitcast.13, bf16[128,1152]{1,0:T(8,128)(2,1)} %images_hbm.1, ...), custom_call_target="tpu_custom_call" | custom-call | tf_op jit(solution)/shard_map/band/pallas_call | solution.py:437
  62.7 1.0 %settle.1 = (f32[128,1152]{1,0:T(8,128)}, f32[128,1152]{1,0:T(8,128)}, f32[1,128]{1,0:T(1,128)}) custom-call(f32[128,1152]{1,0:T(8,128)S(1)} %get-tuple-element.9.image_in, f32[128,1152]{1,0:T(8,128)S(1)} %get-tuple-element.10.text_in, f32[1,128]{1,0:T(1,128)S(1)} %get-tuple-element.11.loss_in), custom_call_target="tpu_custom_call" | custom-call | tf_op jit(solution)/shard_map/settle/pallas_call | solution.py:491

commit v5 on v4

--- a/solution.py
+++ b/solution.py
@@ -291,12 +291,16 @@
         tx_buf[rows, :] = (raw[top:end, :] * text_factor[top:end, :]).astype(BF16)
         tx_near += start_piece(1, tx_buf, piece)
         tx_x.append(to_peer(piece, tx_buf.at[rows], tx_buf.at[pl.ds(PEER * ROWS + piece * PIECE, PIECE)]))
-    id_codes = recv_b2[:, D - HALF : HALF]
-    weigh_in = jnp.where(r_in == 0, 32.0, jnp.where(r_in == 1, 1.0, 0.0)).astype(BF16)
-    tx_cols = dot_t(weigh_in, id_codes) - 1.0
-    tx_ids[0] = tx_cols[0:8, :]
-    tx_near += start_ids(1, tx_ids)
-    tx_x.append(to_peer(2, tx_ids.at[0], tx_ids.at[PEER]))
+        if piece > 0:
+            continue
+        id_codes = recv_b2[:, D - HALF : HALF]
+        weigh_in = jnp.where(r_in == 0, 32.0, jnp.where(r_in == 1, 1.0, 0.0)).astype(BF16)
+        tx_cols = dot_t(weigh_in, id_codes) - 1.0
+        tx_ids[0] = tx_cols[0:8, :]
+        tx_near_ids = start_ids(1, tx_ids)
+        tx_x_ids = to_peer(2, tx_ids.at[0], tx_ids.at[PEER])
+    tx_near += tx_near_ids
+    tx_x.append(tx_x_ids)
     raw_ref[...] = raw
 
     scale = scale_ref[0]
@@ -330,11 +334,6 @@
     col_f = col.astype(F32)
     far_masks = (col_f, 1.0 - col_f)
 
-    for copy in im_far:
-        copy.wait_recv()
-    im_cols = [im_ids[place][0:1, :] for place in range(5)]
-    weights, _ = terms(tx_buf[0:ROWS, :], as_rows(tx_cols[0:1, :]), im_buf[...], im_cols, True, None)
-    text_sum[...] = dot(weights, im_buf[...])
     im_rows = as_rows(im_ids[0][0:1, :])
 
     tx_far, tx_cross, txp = [], [], []
@@ -342,18 +341,24 @@
         tx_far += pass_piece(1, tx_buf, tx_near, piece)
         tx_x[piece].wait_recv()
         if piece == 0:
+            for copy in im_far:
+                copy.wait_recv()
+            im_cols = [im_ids[place][0:1, :] for place in range(5)]
             tx_x[PIECES].wait_recv()
             peer_rows = as_rows(tx_ids[PEER][0:1, :])
         if piece == PIECES - 1:
-            tx_far += pass_ids(1, tx_ids, tx_near)
             for part in range(PIECES):
                 tx_cross += start_piece(2, tx_buf, part, PEER, CROSS)
             tx_cross += start_ids(2, tx_ids, PEER, CROSS)
+            tx_far += pass_ids(1, tx_ids, tx_near)
         top, end = piece * PIECE, (piece + 1) * PIECE
         peer_text = tx_buf[PEER * ROWS + top : PEER * ROWS + end, :]
         weights, _ = terms(peer_text, peer_rows[top:end, :], im_buf[...], im_cols, True, far_masks)
         txp_out[top:end, :] = dot(weights, im_buf[...]).astype(BF16)
         txp.append(to_peer(3 + piece, txp_out.at[pl.ds(top, PIECE)], txp_in.at[pl.ds(top, PIECE)]))
+
+    weights, _ = terms(tx_buf[0:ROWS, :], as_rows(tx_cols[0:1, :]), im_buf[...], im_cols, True, None)
+    text_sum[...] = dot(weights, im_buf[...])
 
     def image_terms(place, blocks):
         cols = tx_buf[place * ROWS : (place + blocks) * ROWS, :]

time: 63.9 us -> 66 us (1.033)
  Pallas kernels: 61.8 us -> 63.8 us
    pallas_call x1, Pallas kernels: 60.7 us -> 62.8 us  [per_device(): pl.pallas_call(kernel, out_shape=(pltpu.VMEM(block, F32), pltpu.VMEM(bloc...]
where the time goes in v5:
time: 66 us; the launch traced here: 65.8 us
  Pallas kernels  63.8 us (97%)
  between operations  1.93 us (3%)
    pallas_call x1, Pallas kernels, per_device(): pl.pallas_call(kernel, out_shape=(pltpu.VMEM(block, F32), pltpu.VMEM(bloc...  62.8 us

profile of v5, /device:TPU:1, one launch (start us, length us, event | category | flops | bytes accessed | tf_op | source)
XLA Modules:
  0.0 65.8 jit_solution(3748885140751063253)
XLA Ops:
  1.9 62.8 %band.1 = (f32[128,1152]{1,0:T(8,128)S(1)}, f32[128,1152]{1,0:T(8,128)S(1)}, f32[1,128]{1,0:T(1,128)S(1)}) custom-call(bf16[288,1152]{1,0:T(8,128)(2,1)} %bitcast.9, s32[1,48]{1,0:T(1,128)} %bitcast.10, s32[1,48]{1,0:T(1,128)} %bitcast.11, s32[1,48]{1,0:T(1,128)} %bitcast.12, s32[1,48]{1,0:T(1,128)} %bitcast.13, bf16[128,1152]{1,0:T(8,128)(2,1)} %images_hbm.1, ...), custom_call_target="tpu_custom_call" | custom-call | tf_op jit(solution)/shard_map/band/pallas_call | solution.py:442
  64.7 1.0 %settle.1 = (f32[128,1152]{1,0:T(8,128)}, f32[128,1152]{1,0:T(8,128)}, f32[1,128]{1,0:T(1,128)}) custom-call(f32[128,1152]{1,0:T(8,128)S(1)} %get-tuple-element.9.image_in, f32[128,1152]{1,0:T(8,128)S(1)} %get-tuple-element.10.text_in, f32[1,128]{1,0:T(1,128)S(1)} %get-tuple-element.11.loss_in), custom_call_target="tpu_custom_call" | custom-call | tf_op jit(solution)/shard_map/settle/pallas_call | solution.py:496
